TPU v7x, 32 devices: a whole 2x2x4 slice. The times are simulated.
32 devices in a mesh: section: 2 (over y), fsdp: 4 (over z), dp: 4 (over x, core).
Axes of the slice: x: 2, y: 2, z: 4, core: 2. Of those that a mesh axis runs over, the one named last changes fastest.
Arguments:
- inputs: bfloat16 [2, 4, 1024, 1536], P(None, 'dp', 'fsdp'), may hold values from -6 to 6
- segment: int32 [2, 4, 1024], P(None, 'dp', 'fsdp'), may hold values from 0 to 2, as said below
- cotangent: bfloat16 [2, 4, 1024, 1536], P(None, 'dp', 'fsdp'), may hold values from -6 to 6
- norm_gain: float32 [2, 1, 1536], P('section'), may hold values from 0.5 to 1.5
- in_weight: bfloat16 [2, 1, 1536, 6448], P('section', None, 'fsdp'), may hold values from -0.15625 to 0.15625
- conv_weight: float32 [2, 1, 4, 3328], P('section'), may hold values from -3 to 3
- conv_bias: float32 [2, 1, 3328], P('section'), may hold values from -3 to 3
- dt_bias: float32 [2, 1, 48], P('section'), may hold values from -7 to -2
- a_log: float32 [2, 1, 48], P('section'), may hold values from -4 to 1
- d_skip: float32 [2, 1, 48], P('section'), may hold values from 0.5 to 1.5
- gate_gain: float32 [2, 1, 3072], P('section'), may hold values from 0.5 to 1.5
- out_weight: bfloat16 [2, 1, 3072, 1536], P('section', None, 'fsdp'), may hold values from -0.109375 to 0.109375
Outputs:
- final: bfloat16 [2, 4, 1024, 1536], P('section', 'dp', 'fsdp')
- input_grad: bfloat16 [2, 4, 1024, 1536], P('section', 'dp', 'fsdp')
- norm_gain_grad: float32 [2, 1, 1536], P('section')
- in_weight_grad: float32 [2, 1, 1536, 6448], P('section', None, 'fsdp')
- conv_weight_grad: float32 [2, 1, 4, 3328], P('section')
- conv_bias_grad: float32 [2, 1, 3328], P('section')
- dt_bias_grad: float32 [2, 1, 48], P('section')
- a_log_grad: float32 [2, 1, 48], P('section')
- d_skip_grad: float32 [2, 1, 48], P('section')
- gate_gain_grad: float32 [2, 1, 3072], P('section')
- out_weight_grad: float32 [2, 1, 3072, 1536], P('section', None, 'fsdp')
Inputs may be any that keep to these rules, and one draw needn't show every extreme that they name: Along each sequence the segment numbers never fall; they start at 0 and end at 2, and segment 1 starts among the first 256 tokens and ends among the last 256.
All inputs are finite; a program needn't handle non-finite values.
Results may differ from a plain program's by a relative error of at most 0.01575.
The roundings to bfloat16 on the way count: a program that leaves them out, or rounds other values in their place, can miss the bound.
Values may be sent and summed in bfloat16 or wider, within the bound.
A program may use at most 384 MiB of HBM per device.

v0:
```python
import jax
import jax.numpy as jnp
from jax import lax
from jax.sharding import PartitionSpec as P

D = 1536
H = 48
P_SIZE = 64
N = 128
K = 4
DI = 3072
DC = 3328
DIN = 6448


EPSILON = 1e-05
HIGHEST = lax.Precision.HIGHEST


def from_behind(value, axis, by):
    peers = lax.axis_size(axis)
    pairs = [(i, i + by) for i in range(peers) if 0 <= i + by < peers]
    return lax.ppermute(value, axis, pairs)


def prefix(value, axis, combine, identity):
    peers, here = (lax.axis_size(axis), lax.axis_index(axis))
    everything = jax.tree.map(lambda part: lax.all_gather(part, axis), value)
    start = jax.tree.map(
        lambda part, zero: jnp.broadcast_to(jnp.asarray(zero, part.dtype), part.shape),
        value,
        identity,
    )

    def prefix_turn(k, before):
        reached = k < here
        new = combine(before, jax.tree.map(lambda part: part[k], everything))
        return jax.tree.map(lambda a, b: jnp.where(reached, a, b), new, before)

    return lax.fori_loop(0, peers, prefix_turn, start)


def carried_in(value, axis, combine, identity):
    peers, here = (lax.axis_size(axis), lax.axis_index(axis))
    everything = jax.tree.map(
        lambda part, kind: lax.all_gather(part.astype(kind), axis),
        value,
        jax.tree.map(lambda a: jnp.bfloat16 if a.dtype == jnp.float32 else a.dtype, value),
    )
    start = jax.tree.map(
        lambda part, zero: jnp.broadcast_to(jnp.asarray(zero, part.dtype), part.shape),
        value,
        identity,
    )

    def carried_turn(k, before):
        at = peers - 1 - k
        reached = at > here
        new = combine(
            before, jax.tree.map(lambda part, own: part[at].astype(own.dtype), everything, value)
        )
        return jax.tree.map(lambda a, b: jnp.where(reached, a, b), new, before)

    return lax.fori_loop(0, peers, carried_turn, start)


def from_behind_2(value, axis, steps):
    count = lax.axis_size(axis)
    pairs = [(source, (source + steps) % count) for source in range(count)]
    return lax.ppermute(value, axis, pairs)


def rms_scale(values, scale_gain):
    return (
        values * lax.rsqrt(jnp.mean(values * values, axis=-1, keepdims=True) + EPSILON) * scale_gain
    )


def state_join(earlier, later):
    return (earlier[0] * later[0], later[0][:, None, None] * earlier[1] + later[1])


def first_half(
    projected, prev_tail, prev_seg, seg_float, conv_w, conv_b, dt_shift, a_logs, skip_gain
):
    row_count = projected.shape[0]
    gate_part = projected[:, :DI]
    padded = jnp.concatenate([prev_tail, projected[:, DI : DI + DC]], axis=0)
    seg_padded = jnp.concatenate([prev_seg, seg_float])
    mixed = conv_b
    for offset in range(K):
        keep_mask = jnp.where(seg_padded[offset : offset + row_count] == seg_float, 1.0, 0.0)
        mixed = mixed + conv_w[offset] * padded[offset : offset + row_count] * keep_mask[:, None]
    conv_out = jax.nn.silu(mixed)
    values = conv_out[:, :DI].reshape(row_count, H, P_SIZE)
    b_matrix = conv_out[:, DI : DI + N]
    c_matrix = conv_out[:, DI + N :]
    step_size = jax.nn.softplus(projected[:, DI + DC :] + dt_shift)
    log_decay = -step_size * jnp.exp(a_logs)
    cumulative = jnp.cumsum(log_decay, axis=0)
    position = lax.broadcasted_iota(jnp.int32, (row_count, row_count), 0)
    source = lax.broadcasted_iota(jnp.int32, (row_count, row_count), 1)
    linked = (seg_float[:, None] == seg_float[None, :]) & (position >= source)
    spread = jnp.where(linked[:, :, None], cumulative[:, None, :] - cumulative[None, :, :], 0.0)
    decay_mat = jnp.where(linked[:, :, None], jnp.exp(spread), 0.0)
    inner = jnp.dot(c_matrix, b_matrix.T, precision=HIGHEST)
    mixing = inner[:, :, None] * decay_mat * step_size[None, :, :]
    intra = (
        jnp.einsum("tsh,shp->thp", mixing, values, precision=HIGHEST) + skip_gain[:, None] * values
    )
    entry = jnp.where(seg_float == prev_seg[-1], 1.0, 0.0)[:, None] * jnp.exp(cumulative)
    weight_out = (
        jnp.where(seg_float == seg_float[-1], 1.0, 0.0)[:, None]
        * jnp.exp(cumulative[-1][None, :] - cumulative)
        * step_size
    )
    local_state = jnp.einsum("sh,shp,sn->hpn", weight_out, values, b_matrix, precision=HIGHEST)
    return (entry[-1], local_state, (intra.reshape(row_count, DI), entry, c_matrix, gate_part))


def second_half(intra, entry, c_matrix, gate_part, state_in, gate_scale):
    row_count = intra.shape[0]
    carried = jnp.einsum("tn,hpn->thp", c_matrix, state_in, precision=HIGHEST) * entry[:, :, None]
    total_mix = intra + carried.reshape(row_count, DI)
    return rms_scale(total_mix * jax.nn.silu(gate_part), gate_scale)


def shards(
    inputs,
    segment,
    cotangent,
    norm_gain,
    in_weight,
    conv_weight,
    conv_bias,
    dt_bias,
    a_log,
    d_skip,
    gate_gain,
    out_weight,
):
    section_index = lax.axis_index("section")
    micro_count = inputs.shape[0]
    tick_count = micro_count + lax.axis_size("section") - 1
    layer_count = in_weight.shape[1]
    row_count = inputs.shape[2]
    in_rows = in_weight.shape[2]
    out_rows = out_weight.shape[2]
    identity = (jnp.ones((H,), jnp.float32), jnp.zeros((H, P_SIZE, N), jnp.float32))

    def fetch(depth_index):
        return (
            lax.all_gather(in_weight[0, depth_index], "fsdp", axis=0, tiled=True),
            lax.all_gather(out_weight[0, depth_index], "fsdp", axis=0, tiled=True),
        )

    def small_params(depth_index):
        return (
            conv_weight[0, depth_index],
            conv_bias[0, depth_index],
            dt_bias[0, depth_index],
            a_log[0, depth_index],
            d_skip[0, depth_index],
        )

    def layer_backward(grad_hidden, saved, seg_row, depth_index):
        hidden, projected, prev_tail, prev_seg, state_in = saved
        full_in, full_out = fetch(depth_index)
        seg_float = seg_row.astype(jnp.float32)

        def local_mixer(proj_float, tail_float, conv_w, conv_b, dt_shift, a_logs, skip_gain):
            return first_half(
                proj_float,
                tail_float,
                prev_seg,
                seg_float,
                conv_w,
                conv_b,
                dt_shift,
                a_logs,
                skip_gain,
            )

        (block_decay, local_state, middle), mixer_back = jax.vjp(
            local_mixer, projected, prev_tail, *small_params(depth_index)
        )
        normed_out, gate_back = jax.vjp(
            second_half,
            middle[0],
            middle[1],
            middle[2],
            middle[3],
            state_in,
            gate_gain[0, depth_index],
        )
        grad_branch = grad_hidden.astype(jnp.bfloat16)
        normed_low = normed_out.astype(jnp.bfloat16)
        grad_normed = lax.dot_general(
            grad_branch, full_out, (((1,), (1,)), ((), ())), preferred_element_type=jnp.float32
        )
        piece = normed_low
        out_share = lax.psum_scatter(
            lax.dot_general(
                piece, grad_branch, (((0,), (0,)), ((), ())), preferred_element_type=jnp.float32
            ).astype(jnp.bfloat16),
            "fsdp",
            scatter_dimension=0,
            tiled=True,
        ).astype(jnp.float32)
        d_intra, d_entry, d_cmat, d_gate, d_state, d_gate_gain = gate_back(grad_normed)
        later_grad = carried_in((block_decay, d_state), "fsdp", state_join, identity)[1]
        d_decay = jnp.sum(later_grad * state_in, axis=(1, 2))
        grads_mixer = mixer_back((d_decay, later_grad, (d_intra, d_entry, d_cmat, d_gate)))
        from_next = from_behind(grads_mixer[1].astype(jnp.bfloat16), "fsdp", -1).astype(jnp.float32)
        grad_proj = (
            grads_mixer[0]
            .at[row_count - (K - 1) :, DI : DI + DC]
            .add(from_next)
            .astype(jnp.bfloat16)
        )
        grad_normed_in = lax.dot_general(
            grad_proj, full_in, (((1,), (1,)), ((), ())), preferred_element_type=jnp.float32
        )
        normed_in, norm_back = jax.vjp(rms_scale, hidden, norm_gain[0, depth_index])
        normed_in_low = normed_in.astype(jnp.bfloat16)
        piece = normed_in_low
        in_share = lax.psum_scatter(
            lax.dot_general(
                piece, grad_proj, (((0,), (0,)), ((), ())), preferred_element_type=jnp.float32
            ).astype(jnp.bfloat16),
            "fsdp",
            scatter_dimension=0,
            tiled=True,
        ).astype(jnp.float32)
        d_hidden, d_norm_gain = norm_back(grad_normed_in)
        small_grads = (
            d_norm_gain,
            grads_mixer[2],
            grads_mixer[3],
            grads_mixer[4],
            grads_mixer[5],
            grads_mixer[6],
            d_gate_gain,
        )
        return (grad_hidden + d_hidden, in_share, out_share, small_grads)

    received = jnp.zeros_like(inputs[0])
    final_recv = received
    final_own = received
    stash = []
    for tick_index in range(tick_count):
        if tick_index < micro_count:
            own_input = inputs[tick_index]
        else:
            own_input = jnp.zeros_like(inputs[0])
        seg_now = jnp.where(
            section_index == 0,
            segment[min(tick_index, micro_count - 1)],
            segment[max(tick_index - 1, 0)],
        )[0]
        hidden = jnp.where(section_index == 0, own_input, received)[0].astype(jnp.float32)
        saved_layers = []
        depth_index = 0
        layer_full_in, layer_full_out = fetch(depth_index)
        normed = rms_scale(hidden, norm_gain[0, depth_index]).astype(jnp.bfloat16)
        layer_projected = jnp.dot(normed, layer_full_in, preferred_element_type=jnp.float32)
        layer_seg_float = seg_now.astype(jnp.float32)
        layer_prev_tail, layer_prev_seg = from_behind(
            (
                layer_projected[row_count - (K - 1) :, DI : DI + DC],
                layer_seg_float[row_count - (K - 1) :],
            ),
            "fsdp",
            1,
        )
        layer_block_decay, layer_local_state, layer_middle = first_half(
            layer_projected,
            layer_prev_tail,
            layer_prev_seg,
            layer_seg_float,
            *small_params(depth_index)
        )
        layer_state_in = prefix(
            (layer_block_decay, layer_local_state), "fsdp", state_join, identity
        )[1]
        layer_normed_out = second_half(
            layer_middle[0],
            layer_middle[1],
            layer_middle[2],
            layer_middle[3],
            layer_state_in,
            gate_gain[0, depth_index],
        )
        branch = jnp.dot(
            layer_normed_out.astype(jnp.bfloat16),
            layer_full_out,
            preferred_element_type=jnp.float32,
        )
        hidden, saved = (
            hidden + branch,
            (hidden, layer_projected, layer_prev_tail, layer_prev_seg, layer_state_in),
        )
        saved_layers.append(saved)
        stash.append((seg_now, saved_layers))
        leaving = hidden.astype(jnp.bfloat16)[None]
        if tick_index < tick_count - 1:
            received = from_behind_2(leaving, "section", 1)
        if tick_index == micro_count - 1:
            final_recv = received
        if tick_index == tick_count - 1:
            final_own = leaving
    final = jnp.where(section_index == 0, final_recv, final_own)[None]
    in_sums = [jnp.zeros((in_rows, DIN), jnp.float32)]
    out_sums = [jnp.zeros((out_rows, D), jnp.float32)]
    small_sums = [None]
    received_grad = jnp.zeros_like(inputs[0])
    grad_recv = received_grad
    grad_own = received_grad
    for back_index in range(tick_count):
        forward_tick = tick_count - 1 - back_index
        micro_last = micro_count - 1 - back_index
        if micro_last >= 0:
            own_grad = cotangent[micro_last]
        else:
            own_grad = jnp.zeros_like(cotangent[0])
        grad_now = jnp.where(section_index == 1, own_grad, received_grad)[0].astype(jnp.float32)
        seg_now, saved_layers = stash[forward_tick]
        for depth_index in reversed(range(layer_count)):
            grad_now, in_share, out_share, small_grads = layer_backward(
                grad_now, saved_layers[depth_index], seg_now, depth_index
            )
            in_sums[depth_index] = in_sums[depth_index] + in_share
            out_sums[depth_index] = out_sums[depth_index] + out_share
            if small_sums[depth_index] is None:
                small_sums[depth_index] = small_grads
            else:
                small_sums[depth_index] = tuple(
                    (total + grad for total, grad in zip(small_sums[depth_index], small_grads))
                )
        leaving_grad = grad_now.astype(jnp.bfloat16)[None]
        if back_index < tick_count - 1:
            received_grad = from_behind_2(leaving_grad, "section", -1)
        if back_index == micro_count - 1:
            grad_recv = received_grad
        if back_index == tick_count - 1:
            grad_own = leaving_grad
    input_grad = jnp.where(section_index == 0, grad_own, grad_recv)[None]
    in_total, out_total = (
        lax.psum(jnp.stack(in_sums).astype(jnp.bfloat16), "dp").astype(jnp.float32),
        lax.psum(jnp.stack(out_sums).astype(jnp.bfloat16), "dp").astype(jnp.float32),
    )
    stacked = [jnp.stack([small_sums[0][member]]) for member in range(7)]
    gain_total, convw_total, convb_total, dtb_total, alog_total, skip_total, gate_total = lax.psum(
        (stacked[0], stacked[1], stacked[2], stacked[3], stacked[4], stacked[5], stacked[6]),
        ("fsdp", "dp"),
    )
    return (
        final,
        input_grad,
        gain_total[None],
        in_total[None],
        convw_total[None],
        convb_total[None],
        dtb_total[None],
        alog_total[None],
        skip_total[None],
        gate_total[None],
        out_total[None],
    )


def solution(mesh):
    return jax.shard_map(
        shards,
        mesh=mesh,
        in_specs=(
            P(None, "dp", "fsdp", None),
            P(None, "dp", "fsdp"),
            P(None, "dp", "fsdp", None),
            P("section", None, None),
            P("section", None, "fsdp", None),
            P("section", None, None, None),
            P("section", None, None),
            P("section", None, None),
            P("section", None, None),
            P("section", None, None),
            P("section", None, None),
            P("section", None, "fsdp", None),
        ),
        out_specs=(
            P("section", "dp", "fsdp", None),
            P("section", "dp", "fsdp", None),
            P("section", None, None),
            P("section", None, "fsdp", None),
            P("section", None, None, None),
            P("section", None, None),
            P("section", None, None),
            P("section", None, None),
            P("section", None, None),
            P("section", None, None),
            P("section", None, "fsdp", None),
        ),
        check_vma=False,
    )
```

profile of v0, /device:TPU:23, one launch (start us, length us, event | category | flops | bytes accessed | tf_op | source)
XLA Modules:
  0.0 3339.5 jit_solution(3871084683587850589)
XLA Ops:
  15.7 331.6 %all-gather.23.cloned.1.call-done = bf16[1,1,1536,6448]{2,3,1,0:T(8,128)(2,1)} async-done(((bf16[1,1,384,6448]{2,3,1,0:T(8,128)(2,1)}), bf16[1,1,1536,6448]{2,3,1,0:T(8,128)(2,1)}) %all-gather.23.cloned.1.call-update) | async-done | bytes 19808272 | tf_op jit(solution)/shard_map/all_gather | solution.py:153
  347.3 10.0 fusion.16
  372.2 10.1 fusion.111
  396.4 106.3 %all-gather.25.cloned.1.call-done = f32[192,64,128]{2,1,0:T(8,128)} async-done(((f32[48,64,128]{2,1,0:T(8,128)}), f32[192,64,128]{2,1,0:T(8,128)}) %all-gather.25.cloned.1.call-update) | async-done | bytes 6291472 | tf_op jit(solution)/shard_map/all_gather | solution.py:28
  502.7 7.5 while.93
  514.1 25.4 fusion.120
  545.4 124.0 %all-gather.27.cloned.1.call-done = bf16[1,1,3072,1536]{3,2,1,0:T(8,128)(2,1)} async-done(((bf16[1,1,768,1536]{3,2,1,0:T(8,128)(2,1)}), bf16[1,1,3072,1536]{3,2,1,0:T(8,128)(2,1)}) %all-gather.27.cloned.1.call-update) | async-done | bytes 9437200 | tf_op jit(solution)/shard_map/all_gather | solution.py:154
  669.3 7.4 fusion.169
  684.3 10.9 collective-permute-done.2
  696.4 10.1 fusion.14
  720.4 10.1 fusion.110
  744.2 107.6 %all-gather.29.cloned.1.call-done = f32[192,64,128]{2,1,0:T(8,128)} async-done(((f32[48,64,128]{2,1,0:T(8,128)}), f32[192,64,128]{2,1,0:T(8,128)}) %all-gather.29.cloned.1.call-update) | async-done | bytes 6291472 | tf_op jit(solution)/shard_map/all_gather | solution.py:28
  851.8 7.6 while.94
  863.5 14.8 fusion.119
  896.6 10.9 collective-permute-done.5
  907.9 8.1 fusion.12
  929.9 10.2 fusion.109
  953.6 107.5 %all-gather.31.cloned.1.call-done = f32[192,64,128]{2,1,0:T(8,128)} async-done(((f32[48,64,128]{2,1,0:T(8,128)}), f32[192,64,128]{2,1,0:T(8,128)}) %all-gather.31.cloned.1.call-update) | async-done | bytes 6291472 | tf_op jit(solution)/shard_map/all_gather | solution.py:28
  1061.1 7.6 while.95
  1072.6 14.7 fusion.118
  1118.0 22.2 fusion.55
  1143.5 24.8 all-gather.33.cloned.1.call-done
  1168.3 11.7 while.96
  1191.5 12.5 bitcast_add_fusion.5
  1204.0 12.8 fusion.387
  1251.7 10.9 scatter-add.10
  1262.7 12.5 fusion.204
  1276.2 18.1 collective-permute-done.9
  1310.2 7.1 all-gather.12
  1322.2 22.2 fusion.57
  1347.8 27.1 all-gather.35.cloned.1.call-done
  1392.8 12.5 bitcast_add_fusion.4
  1405.4 12.6 fusion.386
  1453.0 10.9 scatter-add.11
  1463.9 12.5 fusion.206
  1477.4 18.1 collective-permute-done.11
  1511.0 6.8 convolution_convert_fusion.5
  1519.7 6.6 convolution_convert_fusion.4
  1534.8 12.7 convolution_convert_fusion.2
  1547.5 24.5 copy.320
  1573.2 12.9 convolution_convert_fusion.1
  1586.1 24.7 copy.322
  1611.1 8.1 all-gather.13
  1624.0 22.2 fusion.59
  1649.6 6.8 while.98
  1666.8 12.5 bitcast_add_fusion.3
  1679.4 15.8 fusion.388
  1725.9 10.8 scatter-add.14
  1736.7 12.5 convolution_convert_fusion
  1749.2 24.4 copy.324
  1775.6 7.6 fusion.175
  1784.4 121.0 %reduce-scatter.15.cloned.1.call-done = bf16[768,1536]{1,0:T(8,128)(2,1)} async-done(((bf16[3072,1536]{1,0:T(8,128)(2,1)}), bf16[768,1536]{1,0:T(8,128)(2,1)}) %reduce-scatter.15.cloned.1.call-update) | async-done | bytes 2359312 | tf_op jit(solution)/shard_map/reduce_scatter | solution.py:202
  1905.4 165.1 %reduce-scatter.17.cloned.1.call-done = bf16[768,1536]{1,0:T(8,128)(2,1)} async-done(((bf16[3072,1536]{1,0:T(8,128)(2,1)}), bf16[768,1536]{1,0:T(8,128)(2,1)}) %reduce-scatter.17.cloned.1.call-update) | async-done | bytes 2359312 | tf_op jit(solution)/shard_map/reduce_scatter | solution.py:202
  2075.9 330.7 %reduce-scatter.19.cloned.1.call-done = bf16[384,6448]{1,0:T(8,128)(2,1)} async-done(((bf16[1536,6448]{1,0:T(8,128)(2,1)}), bf16[384,6448]{1,0:T(8,128)(2,1)}) %reduce-scatter.19.cloned.1.call-update) | async-done | bytes 4952080
  2406.6 7.6 copy.321
  2414.2 328.7 %reduce-scatter.21.cloned.1.call-done = bf16[384,6448]{1,0:T(8,128)(2,1)} async-done(((bf16[1536,6448]{1,0:T(8,128)(2,1)}), bf16[384,6448]{1,0:T(8,128)(2,1)}) %reduce-scatter.21.cloned.1.call-update) | async-done | bytes 4952080
  2742.9 7.6 copy.323
  2750.5 328.6 %reduce-scatter.23.cloned.1.call-done = bf16[384,6448]{1,0:T(8,128)(2,1)} async-done(((bf16[1536,6448]{1,0:T(8,128)(2,1)}), bf16[384,6448]{1,0:T(8,128)(2,1)}) %reduce-scatter.23.cloned.1.call-update) | async-done | bytes 4952080
  3079.0 7.6 copy.325
  3086.6 9.4 fusion.96
  3099.3 13.3 fusion.208
  3116.0 116.2 %all-reduce.55.cloned.1.call-done = (bf16[1,1,384,6448]{2,3,1,0:T(8,128)(2,1)}, bf16[1,1,768,1536]{3,2,1,0:T(8,128)(2,1)}) async-done(((bf16[1,1,384,6448]{2,3,1,0:T(8,128)(2,1)}, bf16[1,1,768,1536]{3,2,1,0:T(8,128)(2,1)}), (bf16[1,1,384,6448]{2,3,1,0:T(8,128)(2,1)}, bf16[1,1,768,1536]{3,2,1,0:T(8,128)(2,1)})) %all-reduce.55.cloned.1.call-update) | async-done | bytes 7311376 | tf_op jit(solution)/shard_map/psum | solution.py:349
  3232.2 7.1 broadcast_in_dim.397
  3242.1 81.8 %all-reduce.53.cloned.1.call-done = (f32[1,1,1536]{2,1,0:T(1,128)}, f32[1,1,4,3328]{3,2,1,0:T(4,128)}, f32[1,1,3328]{2,1,0:T(1,128)}, f32[1,1,48]{2,1,0:T(1,128)...) async-done(((f32[1,1,1536]{2,1,0:T(1,128)}, f32[1,1,4,3328]{3,2,1,0:T(4,128)}, f32[1,1,3328]{2,1,0:T(1,128)}, f32[1,1,48]{2,1,0:T(1,128)}, ...) | async-done | bytes 85584 | tf_op jit(solution)/shard_map/psum | solution.py:353
  (887 shorter events, 442.3 us)
Async XLA Ops:
  7.2 340.1 %all-gather.23.cloned.1.call-start = ((), (), s32[]{:S(2)}) async-start(), calls=%async_computation.9 | async-start | bytes 24760320 | tf_op jit(solution)/shard_map/all_gather | solution.py:153
  8.0 494.7 %all-gather.25.cloned.1.call-start = ((), (), s32[]{:S(2)}) async-start(), calls=%async_computation.10 | async-start | bytes 7864320 | tf_op jit(solution)/shard_map/all_gather | solution.py:28
  8.6 348.7 %copy-start.176 = (f32[1,1,256]{2,1,0:T(1,128)}, f32[1,1,256]{2,1,0:T(1,128)S(1)}, u32[]{:S(2)}) copy-start(f32[1,1,256]{2,1,0:T(1,128)S(1)} %get-tuple-element.1042) | copy-start | bytes 3076
  8.7 4.4 collective-permute-start.1
  12.5 895.3 %copy-start.81 = (f32[1536]{0:T(1024)}, f32[1536]{0:T(1024)S(1)}, u32[]{:S(2)}) copy-start(f32[1536]{0:T(1024)S(1)} %reduce.17) | copy-start | bytes 18436
  12.6 359.6 %copy-start.114 = (f32[3328]{0:T(1024)}, f32[3328]{0:T(1024)S(1)}, u32[]{:S(2)}) copy-start(f32[3328]{0:T(1024)S(1)} %reduce.15) | copy-start | bytes 39940
  12.7 707.6 %copy-start.90 = (f32[3328]{0:T(1024)}, f32[3328]{0:T(1024)S(1)}, u32[]{:S(2)}) copy-start(f32[3328]{0:T(1024)S(1)} %get-tuple-element.901) | copy-start | bytes 39940
  12.7 707.6 %copy-start.94 = (f32[3328]{0:T(1024)}, f32[3328]{0:T(1024)S(1)}, u32[]{:S(2)}) copy-start(f32[3328]{0:T(1024)S(1)} %get-tuple-element.902) | copy-start | bytes 39940
  12.8 1204.1 %copy-start.84 = (f32[3328]{0:T(1024)}, f32[3328]{0:T(1024)S(1)}, u32[]{:S(2)}) copy-start(f32[3328]{0:T(1024)S(1)} %get-tuple-element.899) | copy-start | bytes 39940
  12.8 1204.1 %copy-start.87 = (f32[3328]{0:T(1024)}, f32[3328]{0:T(1024)S(1)}, u32[]{:S(2)}) copy-start(f32[3328]{0:T(1024)S(1)} %get-tuple-element.900) | copy-start | bytes 39940
  13.1 350.9 %copy-start.182 = (f32[48]{0:T(128)}, f32[48]{0:T(128)S(1)}, u32[]{:S(2)}) copy-start(f32[48]{0:T(128)S(1)} %exponential_bitcast_fusion) | copy-start | bytes 580
  13.1 334.2 %copy-start.186 = (f32[256]{0:T(256)}, f32[256]{0:T(256)S(1)}, u32[]{:S(2)}) copy-start(f32[256]{0:T(256)S(1)} %fusion.364) | copy-start | bytes 3076
  15.7 350.3 %copy-start.167 = (f32[256]{0:T(256)}, f32[256]{0:T(256)S(1)}, u32[]{:S(2)}) copy-start(f32[256]{0:T(256)S(1)} %get-tuple-element.1055) | copy-start | bytes 3076
  15.7 350.3 %copy-start.217 = (f32[256]{0:T(256)}, f32[256]{0:T(256)S(1)}, u32[]{:S(2)}) copy-start(f32[256]{0:T(256)S(1)} %get-tuple-element.1056) | copy-start | bytes 3076
  361.7 7.9 collective-permute-start
  364.9 149.2 %copy-start.77 = (f32[256,48]{0,1:T(8,128)}, f32[256,48]{0,1:T(8,128)S(1)}, u32[]{:S(2)}) copy-start(f32[256,48]{0,1:T(8,128)S(1)} %get-tuple-element.1006) | copy-start | bytes 147460
  388.8 280.5 %all-gather.27.cloned.1.call-start = ((), (), s32[]{:S(2)}) async-start(), calls=%async_computation.11 | async-start | bytes 11796480 | tf_op jit(solution)/shard_map/all_gather | solution.py:154
  389.6 462.2 %all-gather.29.cloned.1.call-start = ((), (), s32[]{:S(2)}) async-start(), calls=%async_computation.12 | async-start | bytes 7864320 | tf_op jit(solution)/shard_map/all_gather | solution.py:28
  389.8 124.3 %copy-start.133 = (pred[256,256]{1,0:T(8,128)(4,1)}, pred[256,256]{1,0:T(8,128)(4,1)S(1)}, u32[]{:S(2)}) copy-start(pred[256,256]{1,0:T(8,128)(4,1)S(1)} %fusion.284) | copy-start | bytes 196612
  396.4 117.7 %copy-start.115 = (f32[256,256]{1,0:T(8,128)}, f32[256,256]{1,0:T(8,128)S(1)}, u32[]{:S(2)}) copy-start(f32[256,256]{1,0:T(8,128)S(1)} %fusion.330) | copy-start | bytes 786436
  510.2 29.3 copy-start
  539.6 129.8 %copy-start.53 = (bf16[2,1,256,1536]{3,2,1,0:T(8,128)(2,1)S(1)}, bf16[2,1,256,1536]{3,2,1,0:T(8,128)(2,1)}, u32[]{:S(2)}) copy-start(bf16[2,1,256,1536]{3,2,1,0:T(8,128)(2,1)} %param.31) | copy-start | bytes 4718596
  539.6 129.8 %copy-start.68 = (f32[1,1,3072]{2,1,0:T(1,128)S(1)}, f32[1,1,3072]{2,1,0:T(1,128)}, u32[]{:S(2)}) copy-start(f32[1,1,3072]{2,1,0:T(1,128)} %param.41) | copy-start | bytes 36868
  545.3 131.4 %copy-start.223 = (f32[256]{0:T(256)}, f32[256]{0:T(256)S(1)}, u32[]{:S(2)}) copy-start(f32[256]{0:T(256)S(1)} %get-tuple-element.1001) | copy-start | bytes 3076
  545.4 131.4 %copy-start.156 = (f32[256]{0:T(256)}, f32[256]{0:T(256)S(1)}, u32[]{:S(2)}) copy-start(f32[256]{0:T(256)S(1)} %fusion.365) | copy-start | bytes 3076
  676.7 18.5 collective-permute-start.2
  677.1 4.6 collective-permute-start.4
  684.3 30.0 copy-start.169
  684.3 30.0 copy-start.219
  709.5 153.9 %copy-start.79 = (f32[256,48]{0,1:T(8,128)}, f32[256,48]{0,1:T(8,128)S(1)}, u32[]{:S(2)}) copy-start(f32[256,48]{0,1:T(8,128)S(1)} %get-tuple-element.998) | copy-start | bytes 147460
  710.6 7.1 collective-permute-start.3
  737.2 324.0 %all-gather.31.cloned.1.call-start = ((), (), s32[]{:S(2)}) async-start(), calls=%async_computation.13 | async-start | bytes 7864320 | tf_op jit(solution)/shard_map/all_gather | solution.py:28
  737.3 126.0 %copy-start.135 = (pred[256,256]{1,0:T(8,128)(4,1)}, pred[256,256]{1,0:T(8,128)(4,1)S(1)}, u32[]{:S(2)}) copy-start(pred[256,256]{1,0:T(8,128)(4,1)S(1)} %fusion.283) | copy-start | bytes 196612
  744.2 119.2 %copy-start.117 = (f32[256,256]{1,0:T(8,128)}, f32[256,256]{1,0:T(8,128)S(1)}, u32[]{:S(2)}) copy-start(f32[256,256]{1,0:T(8,128)S(1)} %fusion.321) | copy-start | bytes 786436
  863.5 44.3 %slice-start = ((s8[19808256]{0:T(1024)(128)(4,1)}), s8[4194304]{0:T(1024)(128)(4,1)S(1)}, s32[]{:S(2)}) async-start(s8[19808256]{0:T(1024)(128)(4,1)} %bitcast.704), calls=%async_computation.22 | async-start | bytes 8388608
  863.5 44.3 %slice-start.1 = ((s8[19808256]{0:T(1024)(128)(4,1)}), s8[4194304]{0:T(1024)(128)(4,1)S(1)}, s32[]{:S(2)}) async-start(s8[19808256]{0:T(1024)(128)(4,1)} %bitcast.704), calls=%async_computation.23 | async-start | bytes 8388608
  863.5 44.3 %slice-start.2 = ((s8[19808256]{0:T(1024)(128)(4,1)}), s8[4194304]{0:T(1024)(128)(4,1)S(1)}, s32[]{:S(2)}) async-start(s8[19808256]{0:T(1024)(128)(4,1)} %bitcast.704), calls=%async_computation.24 | async-start | bytes 8388608
  889.0 18.4 collective-permute-start.5
  889.4 4.6 collective-permute-start.7
  920.0 7.2 collective-permute-start.6
  946.6 221.7 %all-gather.33.cloned.1.call-start = ((), (), s32[]{:S(2)}) async-start(), calls=%async_computation.14 | async-start | bytes 3932160 | tf_op jit(solution)/shard_map/all_gather | solution.py:46
  946.7 125.8 %copy-start.137 = (pred[256,256]{1,0:T(8,128)(4,1)}, pred[256,256]{1,0:T(8,128)(4,1)S(1)}, u32[]{:S(2)}) copy-start(pred[256,256]{1,0:T(8,128)(4,1)S(1)} %fusion.282) | copy-start | bytes 196612
  953.6 118.9 %copy-start.119 = (f32[256,256]{1,0:T(8,128)}, f32[256,256]{1,0:T(8,128)S(1)}, u32[]{:S(2)}) copy-start(f32[256,256]{1,0:T(8,128)S(1)} %fusion.312) | copy-start | bytes 786436
  1105.9 269.0 %all-gather.35.cloned.1.call-start = ((), (), s32[]{:S(2)}) async-start(), calls=%async_computation.15 | async-start | bytes 3932160 | tf_op jit(solution)/shard_map/all_gather | solution.py:46
  1238.6 8.3 collective-permute-start.8
  1251.7 42.6 %slice-start.11 = ((s8[9437184]{0:T(1024)(128)(4,1)}), s8[1048576]{0:T(1024)(128)(4,1)S(1)}, s32[]{:S(2)}) async-start(s8[9437184]{0:T(1024)(128)(4,1)} %bitcast.710), calls=%async_computation.33 | async-start | bytes 2097152
  1262.7 31.7 slice-start.12
  1262.7 31.7 slice-start.13
  1275.8 18.5 collective-permute-start.9
  1310.0 339.6 %all-gather.37.cloned.1.call-start = ((), (), s32[]{:S(2)}) async-start(), calls=%async_computation.16 | async-start | bytes 3932160 | tf_op jit(solution)/shard_map/all_gather | solution.py:46
  1439.7 8.5 collective-permute-start.10
  1453.0 42.6 %slice-start.14 = ((s8[9437184]{0:T(1024)(128)(4,1)}), s8[1048576]{0:T(1024)(128)(4,1)S(1)}, s32[]{:S(2)}) async-start(s8[9437184]{0:T(1024)(128)(4,1)} %bitcast.712), calls=%async_computation.36 | async-start | bytes 2097152
  1463.9 31.6 slice-start.15
  1463.9 31.6 slice-start.16
  1477.1 18.5 collective-permute-start.11
  1510.9 273.5 %reduce-scatter.13.cloned.1.call-start = ((), (), s32[]{:S(2)}) async-start(), calls=%async_computation.6 | async-start | bytes 11796480 | tf_op jit(solution)/shard_map/reduce_scatter | solution.py:202
  1517.8 387.6 %reduce-scatter.15.cloned.1.call-start = ((), (), s32[]{:S(2)}) async-start(), calls=%async_computation.7 | async-start | bytes 11796480 | tf_op jit(solution)/shard_map/reduce_scatter | solution.py:202
  1526.3 544.2 %reduce-scatter.17.cloned.1.call-start = ((), (), s32[]{:S(2)}) async-start(), calls=%async_computation.8 | async-start | bytes 11796480 | tf_op jit(solution)/shard_map/reduce_scatter | solution.py:202
  1533.7 872.9 %reduce-scatter.19.cloned.1.call-start = ((), (), s32[]{:S(2)}) async-start(), calls=%async_computation.17 | async-start | bytes 25067520
  1572.1 1170.8 %reduce-scatter.21.cloned.1.call-start = ((), (), s32[]{:S(2)}) async-start(), calls=%async_computation.18 | async-start | bytes 25067520
  1610.8 1468.2 %reduce-scatter.23.cloned.1.call-start = ((), (), s32[]{:S(2)}) async-start(), calls=%async_computation.19 | async-start | bytes 25067520
  1713.3 8.4 collective-permute-start.12
  1773.6 1458.6 %all-reduce.55.cloned.1.call-start = ((), (), s32[]{:S(2)}) async-start(), calls=%async_computation.21 | async-start | bytes 14622720 | tf_op jit(solution)/shard_map/psum | solution.py:349
  3096.1 227.9 %all-reduce.53.cloned.1.call-start = ((), (), s32[]{:S(2)}) async-start(), calls=%async_computation.20 | async-start | bytes 173056 | tf_op jit(solution)/shard_map/psum | solution.py:353
  (235 other events, 1993.0 us)
Sparse Core Ops, SparseCore 0:
  9.7 337.5 all-gather.22
  389.0 113.6 all-gather.24
  504.3 165.0 all-gather.26
  737.3 114.4 all-gather.28
  946.7 114.4 all-gather.30
  1106.1 62.1 all-gather.32
  1310.1 64.7 all-gather.34
  1511.1 64.7 all-gather.36
  1578.2 162.7 reduce-scatter.12
  1743.3 162.1 reduce-scatter.14
  1908.4 162.1 reduce-scatter.16
  2072.7 333.8 reduce-scatter.18
  2409.0 333.8 reduce-scatter.20
  2745.1 333.8 reduce-scatter.22
  3096.2 135.9 all-reduce.54
  3237.5 86.3 all-reduce.52
where the time goes:
time: 3360 us; the launch traced here: 3340 us
  waiting for transfers between devices  2360 us (70%)
  matrix products  403 us (12%)
  other arithmetic  268 us (8%)
  local copies, waits for them, and re-layouts  224 us (7%)
  blocking collectives  36.9 us (1%)
    unnamed x19, waiting for transfers between devices  990 us
    all_gather x1, waiting for transfers between devices, fetch(): lax.all_gather(in_weight[0, depth_index], 'fsdp', axis=0, tiled=True)  332 us
    all_gather x3, waiting for transfers between devices, prefix(): everything = jax.tree.map(lambda part: lax.all_gather(part, axis), value)  321 us
    reduce_scatter x3, waiting for transfers between devices, layer_backward(): lax.psum_scatter(lax.dot_general(piece, grad_branch, (((0,), (0,)), ((),...  286 us
    dot_general x9, matrix products, first_half(): jnp.einsum('tsh,shp->thp', mixing, values, precision=HIGHEST)  159 us
    unnamed x556, local copies, waits for them, and re-layouts  137 us
    all_gather x1, waiting for transfers between devices, fetch(): lax.all_gather(out_weight[0, depth_index], 'fsdp', axis=0, tiled=True)  124 us
    psum x1, waiting for transfers between devices, shards(): lax.psum(jnp.stack(in_sums).astype(jnp.bfloat16), 'dp').astype(jnp.float32)  116 us
  transfers between devices with their start and end apart: 29, of which 20 were waited for; matrix products, arithmetic and copies ran while one was open for 13% of the time, Pallas kernels for 0%

commit v1 on v0

v1 whole, which is shorter than its diff:
```python
import functools

import jax
import jax.numpy as jnp
from jax import lax
from jax.experimental import pallas as pl
from jax.experimental.pallas import tpu as pltpu
from jax.sharding import PartitionSpec as P

D = 1536
H = 48
P_SIZE = 64
N = 128
K = 4
DI = 3072
DC = 3328
DIN = 6448
EPSILON = 1e-05
HIGHEST = lax.Precision.HIGHEST
BF16 = jnp.bfloat16
F32 = jnp.float32
Q = 128
LANES = 128


def dot(a, b, dims=((1,), (0,)), precision=None):
    return lax.dot_general(a, b, (dims, ((), ())), preferred_element_type=F32, precision=precision)


def low_dot(a, b, dims=((1,), (0,))):
    return dot(a.astype(BF16), b.astype(BF16), dims)


def fine_dot(a, b, dims=((1,), (0,))):
    return dot(a, b, dims, HIGHEST)


def pair_lanes(table, first, low_half):
    return jnp.where(low_half, table[:, first : first + 1], table[:, first + 1 : first + 2])


def decay_tables(proj_dt, dt_bias, a_row, tri):
    shifted = proj_dt + dt_bias
    step = jnp.maximum(shifted, 0.0) + jnp.log1p(jnp.exp(-jnp.abs(shifted)))
    log_decay = -step * jnp.exp(a_row)
    cumulative = fine_dot(tri, log_decay)
    return shifted, step, log_decay, cumulative


def triangles():
    row = lax.broadcasted_iota(jnp.int32, (Q, Q), 0)
    column = lax.broadcasted_iota(jnp.int32, (Q, Q), 1)
    return row, column


MESH_ID = pl.DeviceIdType.MESH
VMEM_LIMIT = 60 * 1024 * 1024


def remote(src, dst, send_sem, recv_sem, device):
    return pltpu.make_async_remote_copy(
        src_ref=src, dst_ref=dst, send_sem=send_sem, recv_sem=recv_sem, device_id=device, device_id_type=MESH_ID
    )


def greet(devices):
    barrier = pltpu.get_barrier_semaphore()
    count = 0
    for condition, device in devices:
        if condition is None:
            pl.semaphore_signal(barrier, inc=1, device_id=device, device_id_type=MESH_ID)
            count = count + 1
        else:

            @pl.when(condition)
            def _():
                pl.semaphore_signal(barrier, inc=1, device_id=device, device_id_type=MESH_ID)

            count = count + condition.astype(jnp.int32)
    pl.semaphore_wait(barrier, count)


def bits_of(peers):
    return [1 << k for k in range(peers.bit_length() - 1)]


def has_bit(value, bit):
    return (value // bit) % 2


def flip(value, bits):
    bit = 1
    out = value
    while bit <= bits:
        if bits & bit:
            out = out + bit * (1 - 2 * has_bit(value, bit))
        bit = bit * 2
    return out


def to_column(row):
    down, across = triangles()
    return jnp.sum(jnp.where(down == across, jnp.broadcast_to(row, (Q, Q)), 0.0), axis=1, keepdims=True)


def to_row(column):
    down, across = triangles()
    return jnp.sum(jnp.where(down == across, jnp.broadcast_to(column, (Q, Q)), 0.0), axis=0, keepdims=True)


def group_tiles(tiles, send_sem, recv_sem, here, peers):
    copies = [
        remote(tiles.at[0], tiles.at[j], send_sem.at[j], recv_sem.at[j], {"dp": flip(here, j)})
        for j in range(1, peers)
    ]
    for copy in copies:
        copy.start()
    for copy in copies:
        copy.wait()
    total = tiles[0]
    for j in range(1, peers):
        total = total + tiles[j]
    return total


class GroupRows:

    def __init__(self, where, here, peers, send_sem, recv_sem):
        self.where, self.here, self.peers = where, here, peers
        self.send_sem, self.recv_sem = send_sem, recv_sem

    def part(self, j):
        return self.where(flip(self.here, j))

    def copy(self, j, bit, source=None):
        part = self.part(j)
        return remote(
            part if source is None else source, part, self.send_sem.at[j ^ bit], self.recv_sem.at[j ^ bit],
            {"dp": flip(self.here, bit)},
        )

    def begin(self, source=None):
        for bit in bits_of(self.peers)[::-1]:
            self.copy(0, bit, source).start()

    def finish(self):
        for bit in bits_of(self.peers)[::-1]:
            for j in range(bit, self.peers, 2 * bit):
                self.copy(j ^ bit, bit).wait_send()
                landing = self.part(j)
                remote(
                    landing, landing, self.send_sem.at[j], self.recv_sem.at[j], {"dp": flip(self.here, bit)}
                ).wait_recv()
                for lower in bits_of(bit)[::-1]:
                    self.copy(j, lower).start()


def rows_of(whole, rows):
    return lambda device: whole.at[pl.ds(pl.multiple_of(device * rows, 8), rows)]


class GroupSum:

    def __init__(self, partial, landed, per_rank, here, peers, send_sem, recv_sem):
        self.partial, self.landed, self.per_rank = partial, landed, per_rank
        self.here, self.bits = here, bits_of(peers)
        self.send_sem, self.recv_sem = send_sem, recv_sem

    def leaves_by(self, k, piece):
        owner = piece // self.per_rank
        fits = has_bit(owner, self.bits[k]) != has_bit(self.here, self.bits[k])
        for bit in self.bits[:k]:
            fits = fits & (has_bit(owner, bit) == has_bit(self.here, bit))
        return fits

    def copy(self, k, piece):
        rows = pl.ds(pl.multiple_of(piece * Q, Q), Q)
        return remote(
            self.partial.at[rows], self.landed.at[k, rows], self.send_sem.at[k, piece], self.recv_sem.at[k, piece],
            {"dp": flip(self.here, self.bits[k])},
        )

    def send(self, k, piece):
        @pl.when(self.leaves_by(k, piece))
        def _():
            if k > 0:
                rows = pl.ds(pl.multiple_of(piece * Q, Q), Q)
                total = self.partial[rows, :].astype(F32)
                for m in range(k):
                    self.copy(m, piece).wait_recv()
                    total = total + self.landed[m, rows, :].astype(F32)
                self.partial[rows, :] = total.astype(BF16)
            self.copy(k, piece).start()

    def own(self, piece):
        rows = pl.ds(pl.multiple_of(piece * Q, Q), Q)
        total = self.partial[rows, :].astype(F32)
        for m in range(len(self.bits)):
            self.copy(m, piece).wait_recv()
            total = total + self.landed[m, rows, :].astype(F32)
        return total

    def settle(self, pieces):
        for k in range(len(self.bits)):
            for piece in range(pieces):

                @pl.when(self.leaves_by(k, piece))
                def _():
                    self.copy(k, piece).wait_send()


def rms_parts(values):
    return lax.rsqrt(jnp.mean(values * values, axis=-1, keepdims=True) + EPSILON)


class SectionGather:

    def __init__(self, held, section, nf, y, z, sems):
        self.held, self.section, self.nf, self.y, self.z, self.sems = held, section, nf, y, z, sems
        width = held.shape[1]
        first = -(-width // 32) * 16
        self.spans = [(0, first), (first, width - first)]
        self.peer = {"section": 1 - y}

    def block(self, b, part):
        start, size = self.spans[part]
        return self.held.at[b, pl.ds(start, size)]

    def each(self, body):
        for part in range(2):
            owner = self.y == self.section

            @pl.when(owner if part == 0 else jnp.logical_not(owner))
            def _():
                body(part)

    def send(self, b, part, row, k, landed, device):
        here = self.block(b, part)
        return remote(here, here, self.sems.at[row, k], self.sems.at[landed, k], device)

    def right(self, k, b, part):
        return self.send(b, part, 0, k, 2, {"fsdp": self.z + 1})

    def left(self, k, b, part):
        return self.send(b, part, 1, k, 3, {"fsdp": self.z - 1})

    def over(self, k, b, part):
        return self.send(b, part, 4, k, 5, self.peer)

    def cross(self):
        here = self.block(self.z, 1)
        return remote(here, here, self.sems.at[6, 0], self.sems.at[6, 1], self.peer)

    def has_right(self):
        return self.z < self.nf - 1

    def has_left(self):
        return self.z > 0

    def start_cross(self):
        @pl.when(self.y == self.section)
        def _():
            self.cross().start()

    def begin(self):
        def body(part):
            if part == 1:
                self.cross().wait_recv()

            @pl.when(self.has_right())
            def _():
                self.right(1, self.z, part).start()

            @pl.when(self.has_left())
            def _():
                self.left(1, self.z, part).start()

            if part == 0:
                self.cross().wait_send()
                self.over(0, self.z, 0).start()

        self.each(body)

    def settle_begin(self):
        def body(part):
            @pl.when(self.has_right())
            def _():
                self.right(1, self.z, part).wait_send()

            @pl.when(self.has_left())
            def _():
                self.left(1, self.z, part).wait_send()

            if part == 0:
                self.over(0, self.z, 0).wait_send()
            else:
                self.over(0, self.z, 0).wait_recv()

        self.each(body)

    def sides(self, k, body):
        @pl.when(self.z >= k)
        def _():
            body(self.z - k, k, True)

        @pl.when(self.z + k < self.nf)
        def _():
            body(self.z + k, self.nf + k, False)

    def arrive(self, k):
        def body(part):
            def one(b, index, from_left):
                if from_left:
                    self.right(k, b, part).wait_recv()
                else:
                    self.left(k, b, part).wait_recv()

            self.sides(k, one)

        self.each(body)

    def relay(self, k):
        def body(part):
            def one(b, index, from_left):
                if k < self.nf - 1:
                    if from_left:

                        @pl.when(self.has_right())
                        def _():
                            self.right(k + 1, b, part).start()

                    else:

                        @pl.when(self.has_left())
                        def _():
                            self.left(k + 1, b, part).start()

                self.over(index, b, part).start()

            self.sides(k, one)

        self.each(body)

    def settle(self, k):
        def body(part):
            def one(b, index, from_left):
                self.over(index, b, part).wait_send()
                self.over(index, b, 1 - part).wait_recv()
                if k < self.nf - 1:
                    if from_left:

                        @pl.when(self.has_right())
                        def _():
                            self.right(k + 1, b, part).wait_send()

                    else:

                        @pl.when(self.has_left())
                        def _():
                            self.left(k + 1, b, part).wait_send()

            self.sides(k, one)

        self.each(body)


class OutGather:

    def __init__(self, source, held, section, nf, y, z, d, sems):
        self.source, self.held, self.section, self.nf = source, held, section, nf
        self.y, self.z, self.d, self.sems = y, z, d, sems
        self.pieces = sems.shape[1]
        self.rows = source.shape[0] // self.pieces
        self.columns = source.shape[1] // 2
        self.peer = {"section": 1 - y}
        self.source_here = z == d

    def owner(self):
        return self.y == self.section

    def piece(self, ref, part, i):
        return ref.at[pl.ds(i * self.rows, self.rows), pl.ds(part * self.columns, self.columns)]

    def send(self, i, part, row, landed, device, source=None):
        target = self.piece(self.held, part, i)
        return remote(
            target if source is None else self.piece(source, part, i), target, self.sems.at[row, i],
            self.sems.at[landed, i], device,
        )

    def right(self, i, part, source=None):
        return self.send(i, part, 0, 2, {"fsdp": self.z + 1}, source)

    def left(self, i, part, source=None):
        return self.send(i, part, 1, 2, {"fsdp": self.z - 1}, source)

    def over(self, i, part, source=None):
        return self.send(i, part, 3, 4, self.peer, source)

    def cross(self):
        columns = pl.ds(self.columns, self.columns)
        return remote(
            self.source.at[:, columns], self.held.at[:, columns], self.sems.at[5, 0], self.sems.at[5, 1], self.peer
        )

    def keep(self):
        return pltpu.make_async_copy(self.source, self.held, self.sems.at[5, 2])

    def goes_right(self):
        return (self.z >= self.d) & (self.z < self.nf - 1)

    def goes_left(self):
        return (self.z <= self.d) & (self.z > 0)

    def each(self, condition, body):
        for part in range(2):
            mine = self.owner() if part == 0 else jnp.logical_not(self.owner())

            @pl.when(condition & mine)
            def _():
                body(part)

    def along(self, i, part, action, source=None):
        @pl.when(self.goes_right())
        def _():
            action(self.right(i, part, source))

        @pl.when(self.goes_left())
        def _():
            action(self.left(i, part, source))

    def begin(self):
        @pl.when(self.source_here & self.owner())
        def _():
            self.cross().start()
            self.keep().start()
            for i in range(self.pieces):
                self.along(i, 0, lambda copy: copy.start(), self.source)
            for i in range(self.pieces):
                self.over(i, 0, self.source).start()

    def begin_other(self):
        @pl.when(self.source_here & jnp.logical_not(self.owner()))
        def _():
            self.cross().wait_recv()
            for i in range(self.pieces):
                self.along(i, 1, lambda copy: copy.start())

    def hops(self, distance):
        def body(part):
            for i in range(self.pieces):
                self.right(i, part).wait_recv()
                self.along(i, part, lambda copy: copy.start())
                self.over(i, part).start()

        self.each((self.z == self.d + distance) | (self.z == self.d - distance), body)

    def settle(self):
        @pl.when(self.source_here & self.owner())
        def _():
            self.cross().wait_send()
            self.keep().wait()

        def at_source(part):
            for i in range(self.pieces):
                self.along(i, part, lambda copy: copy.wait_send())
                if part == 0:
                    self.over(i, 0).wait_send()
                else:
                    self.over(i, 0).wait_recv()

        def elsewhere(part):
            for i in range(self.pieces):
                self.along(i, part, lambda copy: copy.wait_send())
                self.over(i, part).wait_send()
                self.over(i, 1 - part).wait_recv()

        self.each(self.source_here, at_source)
        self.each(jnp.logical_not(self.source_here), elsewhere)


def line_neighbours(nf, y, z):
    return [
        (None, {"section": 1 - y}),
        (z < nf - 1, {"fsdp": z + 1}),
        (z > 0, {"fsdp": z - 1}),
    ]


def start_kernel(
    nf, nd, rows, x_ref, seg_ref, in_ref, out_ref, conv_w_ref, conv_b_ref, norm_ref, gate_ref, head_ref,
    hidden_ref, normed_all, w_in0, w_in1, w_out0, seg_out,
    conv_w_out, conv_b_out, dtb_out, alog_out, skip_out, gain_out, norm_out, meta_out,
    table, x_low, normed_low, seg_all, local_sem, swap_send, swap_recv, small_sem, in_sems0, in_sems1, out_sems,
    own_sem, group_send, group_recv,
):
    y, z, d = lax.axis_index("section"), lax.axis_index("fsdp"), lax.axis_index("dp")
    ch = DI // nd
    heads = H // nd
    lines = rows // Q * 8
    length = rows * nd
    twin = {"fsdp": d, "dp": z}
    peer = {"section": 1 - y}
    home = z == d
    away = z != d
    greet(line_neighbours(nf, y, z) + [(away, twin)] + [(None, {"dp": flip(d, bit)}) for bit in bits_of(nd)])
    gathers = [SectionGather(w_in0, 0, nf, y, z, in_sems0), SectionGather(w_in1, 1, nf, y, z, in_sems1)]
    outs = OutGather(out_ref, w_out0, 0, nf, y, z, d, out_sems)

    def own(held):
        return [
            pltpu.make_async_copy(
                in_ref.at[pl.ds(pl.multiple_of(begin, 16), count)], held.at[z, pl.ds(place, count)], own_sem.at[k]
            )
            for k, (begin, place, count) in enumerate(
                [(d * ch, 0, ch), (DI + d * ch, ch, ch), (2 * DI, 2 * ch, DIN - 2 * DI)]
            )
        ]

    for section, held in enumerate((w_in0, w_in1)):

        @pl.when(y == section)
        def _():
            for copy in own(held):
                copy.start()
            for copy in own(held):
                copy.wait()

    gathers[0].start_cross()
    gathers[1].start_cross()

    table[y, 0:4, :] = conv_w_ref[...]
    table[y, 4:5, :] = conv_b_ref[...]
    table[y, 5:6, 0:D] = norm_ref[...]
    table[y, 6:7, 0:DI] = gate_ref[...]
    for k in range(3):
        table[y, 7:8, k * LANES : (k + 1) * LANES] = head_ref[k : k + 1, :]
    small_copy = remote(table.at[y], table.at[y], small_sem.at[0], small_sem.at[1], peer)
    small_copy.start()

    def seg_rows(device):
        return seg_all.at[pl.ds(pl.multiple_of(device * lines, 8), lines)]

    swaps = [
        remote(x_ref.at[y], hidden_ref, swap_send.at[0], swap_recv.at[0], twin),
        remote(seg_ref, seg_rows(z), swap_send.at[1], swap_recv.at[1], twin),
    ]
    stays = [
        pltpu.make_async_copy(x_ref.at[y], hidden_ref, local_sem.at[1]),
        pltpu.make_async_copy(seg_ref, seg_rows(d), local_sem.at[2]),
    ]

    @pl.when(away)
    def _():
        for copy in swaps:
            copy.start()

    @pl.when(home)
    def _():
        for copy in stays:
            copy.start()

    gathers[0].begin()
    outs.begin()

    def settle_swap(k):
        @pl.when(away)
        def _():
            swaps[k].wait()

        @pl.when(home)
        def _():
            stays[k].wait()

    small_copy.wait()
    settle_swap(0)
    x_copy = pltpu.make_async_copy(hidden_ref, x_low, local_sem.at[1])
    x_copy.start()
    x_copy.wait()
    values = x_low[...].astype(F32)
    normed_low[...] = (values * rms_parts(values) * table[0, 5:6, 0:D]).astype(BF16)
    normed_group = GroupRows(rows_of(normed_all, rows), d, nd, group_send.at[0], group_recv.at[0])
    normed_own = pltpu.make_async_copy(normed_low, normed_group.part(0), local_sem.at[0])
    normed_own.start()
    normed_group.begin(normed_low)
    settle_swap(1)
    seg_group = GroupRows(seg_rows, d, nd, group_send.at[1], group_recv.at[1])
    seg_group.begin()

    turn = d * heads
    low_half = lax.broadcasted_iota(jnp.int32, (1, LANES), 1) < P_SIZE
    channels = pl.ds(pl.multiple_of(d * ch, LANES), ch)
    for section in range(2):
        conv_w_out[section, :, 0:ch] = table[section, 0:4, channels]
        conv_w_out[section, :, ch:] = table[section, 0:4, DI:DC]
        conv_b_out[section, :, 0:ch] = table[section, 4:5, channels]
        conv_b_out[section, :, ch:] = table[section, 4:5, DI:DC]
        norm_out[section] = table[section, 5:6, 0:D]
        gain_out[section] = table[section, 6:7, channels]
        head_rows = [
            pltpu.roll(table[section, :, k * LANES : (k + 1) * LANES], LANES - turn, 1)[7:8, :] for k in range(3)
        ]
        dtb_out[section] = head_rows[0]
        alog_out[section] = head_rows[1]
        for pair in range(ch // LANES):
            skip_out[section, :, pair * LANES : (pair + 1) * LANES] = pair_lanes(head_rows[2], 2 * pair, low_half)

    gathers[0].arrive(1)
    gathers[0].relay(1)
    outs.begin_other()
    outs.hops(1)
    for k in range(2, nf):
        gathers[0].arrive(k)
        gathers[0].relay(k)
        if k == 2:
            gathers[1].begin()
            normed_group.finish()
            seg_group.finish()
            normed_own.wait()
        outs.hops(k)

    seg_copy = pltpu.make_async_copy(seg_all, seg_out, local_sem.at[0])
    seg_copy.start()
    lane = lax.broadcasted_iota(jnp.int32, (8, LANES), 1)
    sub_lane = lax.broadcasted_iota(jnp.int32, (Q, LANES), 1)
    before = jnp.full((8, LANES), -1.0, F32)
    for chunk in range(length // Q):
        now = seg_all[chunk * 8 : chunk * 8 + 8, :]
        columns = [now[0:1, :]]
        for lag in range(1, K):
            earlier = jnp.where(lane < lag, pltpu.roll(before, lag, 1), pltpu.roll(now, lag, 1))
            columns.append(jnp.where(earlier == now, 1.0, 0.0)[0:1, :])
        columns.append(jnp.where(now == before[:, Q - 1 : Q], 1.0, 0.0)[0:1, :])
        columns.append(jnp.where(now == now[:, Q - 1 : Q], 1.0, 0.0)[0:1, :])
        block = jnp.zeros((Q, LANES), F32)
        for k, row in enumerate(columns):
            block = jnp.where(sub_lane == k, to_column(row), block)
        meta_out[chunk * Q : (chunk + 1) * Q, :] = block
        before = now

    gathers[1].arrive(1)
    for k in range(1, nf):
        gathers[0].settle(k)
    gathers[0].settle_begin()
    gathers[1].settle_begin()
    outs.settle()
    seg_copy.wait()


def run_start(nf, nd, rows, x, seg, in_rows, out_rows, conv_w, conv_b, norm_gain, gate_gain, head_table):
    length = rows * nd
    ch = DI // nd
    conv_width = ch + 2 * N
    block = in_rows.shape[1]
    width = 2 * ch + DIN - 2 * DI
    lines = seg.shape[0]
    anywhere = pl.BlockSpec(memory_space=pl.ANY)
    local = pl.BlockSpec(memory_space=pltpu.VMEM)
    dma = pltpu.SemaphoreType.DMA
    return pl.pallas_call(
        functools.partial(start_kernel, nf, nd, rows),
        in_specs=[anywhere] * 4 + [local] * 5,
        out_specs=[anywhere] * 6 + [local] * 8,
        out_shape=[
            jax.ShapeDtypeStruct((rows, D), BF16),
            jax.ShapeDtypeStruct((length, D), BF16),
            jax.ShapeDtypeStruct((nf, width, block), BF16),
            jax.ShapeDtypeStruct((nf, width, block), BF16),
            jax.ShapeDtypeStruct((ch, D), BF16),
            jax.ShapeDtypeStruct((lines * nd, LANES), F32),
            jax.ShapeDtypeStruct((2, K, conv_width), F32),
            jax.ShapeDtypeStruct((2, 1, conv_width), F32),
            jax.ShapeDtypeStruct((2, 1, LANES), F32),
            jax.ShapeDtypeStruct((2, 1, LANES), F32),
            jax.ShapeDtypeStruct((2, 1, ch), F32),
            jax.ShapeDtypeStruct((2, 1, ch), F32),
            jax.ShapeDtypeStruct((2, 1, D), F32),
            jax.ShapeDtypeStruct((length, LANES), F32),
        ],
        scratch_shapes=[
            pltpu.VMEM((2, 8, DC), F32),
            pltpu.VMEM((rows, D), BF16),
            pltpu.VMEM((rows, D), BF16),
            pltpu.VMEM((lines * nd, LANES), F32),
            dma((3,)),
            dma((2,)),
            dma((2,)),
            dma((2,)),
            dma((7, 2 * nf)),
            dma((7, 2 * nf)),
            dma((6, 4)),
            dma((3,)),
            dma((2, nd)),
            dma((2, nd)),
        ],
        compiler_params=pltpu.CompilerParams(
            vmem_limit_bytes=VMEM_LIMIT, collective_id=1, has_side_effects=True
        ),
        name="gather_start",
    )(x, seg, in_rows, out_rows, conv_w, conv_b, norm_gain, gate_gain, head_table)


class SectionSum:

    def __init__(self, view, nf, y, z, own, landed, chain, sems, result):
        self.view, self.nf, self.y, self.z, self.result = view, nf, y, z, result
        self.own, self.landed, self.chain = own, landed, chain
        self.load_sem, self.over_send, self.over_recv, self.chain_send, self.chain_recv = (
            sems.at[0], sems.at[1], sems.at[2], sems.at[3], sems.at[4]
        )
        self.part_rows = own.shape[1]

    def load(self, block):
        return pltpu.make_async_copy(self.view(block, self.y), self.own.at[block], self.load_sem.at[block])

    def over(self, block):
        return remote(
            self.view(block, 1 - self.y), self.landed.at[block], self.over_send.at[block], self.over_recv.at[block],
            {"section": 1 - self.y},
        )

    def right(self, block):
        return remote(
            self.own.at[block], self.chain.at[block], self.chain_send.at[block], self.chain_recv.at[block],
            {"fsdp": self.z + 1},
        )

    def left(self, block, arrives):
        slot = self.nf if arrives else block
        return remote(
            self.own.at[block], self.chain.at[slot], self.chain_send.at[block], self.chain_recv.at[slot],
            {"fsdp": self.z - 1},
        )

    def at(self, k, body):
        if k == 0:
            body(self.z, False)
            return

        @pl.when(self.z + k < self.nf)
        def _():
            body(self.z + k, True)

        @pl.when(self.z - k >= 0)
        def _():
            body(self.z - k, False)

    def begin(self):
        self.at(self.nf - 1, lambda block, rightward: self.over(block).start())
        for k in range(self.nf - 1, -1, -1):
            self.at(k, lambda block, rightward: self.load(block).start())

    def add(self, block, sources, target):
        step = 32

        def some(i, carry):
            rows = pl.ds(pl.multiple_of(i * step, 16), step)
            total = self.own[block, rows, :].astype(F32)
            for ref, slot in sources:
                total = total + ref[slot, rows, :].astype(F32)
            if target is None:
                self.own[block, rows, :] = total.astype(BF16)
            else:
                target[rows, :] = total.astype(BF16)
            return carry

        lax.fori_loop(0, self.part_rows // step, some, 0)

    def ready(self, block):
        self.load(block).wait()
        self.over(block).wait_recv()

    def stage(self, k):
        z, nf = self.z, self.nf
        self.at(k, lambda block, rightward: self.ready(block))
        self.at(k - 1, lambda block, rightward: self.over(block).start())

        def one(block, rightward):
            far_end = z == 0 if rightward else z == nf - 1
            arrived = self.right(block) if rightward else self.left(block, False)
            leaving = self.right(block) if rightward else self.left(block, k == 1)

            @pl.when(jnp.logical_not(far_end))
            def _():
                arrived.wait_recv()
                self.add(block, [(self.landed, block), (self.chain, block)], None)

            @pl.when(far_end)
            def _():
                self.add(block, [(self.landed, block)], None)

            leaving.start()

        self.at(k, one)

    def finish(self):
        z, nf, target = self.z, self.nf, self.result
        self.ready(z)

        @pl.when(z > 0)
        def _():
            self.right(z).wait_recv()

        @pl.when(z < nf - 1)
        def _():
            self.left(z, True).wait_recv()

        @pl.when(z == 0)
        def _():
            self.add(z, [(self.landed, z), (self.chain, nf)], target)

        @pl.when(z == nf - 1)
        def _():
            self.add(z, [(self.landed, z), (self.chain, z)], target)

        @pl.when((z > 0) & (z < nf - 1))
        def _():
            self.add(z, [(self.landed, z), (self.chain, z), (self.chain, nf)], target)

    def settle(self):
        z, nf = self.z, self.nf
        self.over(z).wait_send()
        for k in range(nf - 1, 0, -1):

            @pl.when(z + k < nf)
            def _():
                self.over(z + k).wait_send()
                self.right(z + k).wait_send()

            @pl.when(z - k >= 0)
            def _():
                self.over(z - k).wait_send()
                self.left(z - k, k == 1).wait_send()


def in_parts(width):
    rows = -(-width // 64) * 32
    return rows, width - rows


def in_view(source, nf):
    rows, second = in_parts(source.shape[-2])

    def view(block, part):
        here = pl.ds(pl.multiple_of(part * second, 16), rows)
        if len(source.shape) == 3:
            return source.at[block, here]
        columns = source.shape[1] // nf
        return source.at[here, pl.ds(pl.multiple_of(block * columns, LANES), columns)]

    return view


def out_view(source, nf):
    rows, columns = source.shape[0] // nf, source.shape[1] // 2

    def view(block, part):
        here = pl.ds(pl.multiple_of(block * rows, 16), rows)
        return source.at[here, pl.ds(pl.multiple_of(part * columns, LANES), columns)]

    return view


def in_part_shape(nf, source):
    columns = source.shape[2] if len(source.shape) == 3 else source.shape[1] // nf
    return in_parts(source.shape[-2])[0], columns


def out_part_shape(nf, source):
    return source.shape[0] // nf, source.shape[1] // 2


def section_sum_scratch(nf, part):
    return [
        pltpu.VMEM((nf,) + part, BF16),
        pltpu.VMEM((nf,) + part, BF16),
        pltpu.VMEM((nf + 1,) + part, BF16),
        pltpu.SemaphoreType.DMA((5, nf + 1)),
        pltpu.VMEM(part, BF16),
    ]


class SectionReturn:

    def __init__(self, piece, place, owner, y, sems):
        self.piece, self.place, self.owner, self.y, self.sems = piece, place, owner, y, sems

    def keep(self):
        return pltpu.make_async_copy(self.piece(self.owner), self.place(self.owner), self.sems.at[2])

    def send(self):
        other = 1 - self.owner
        return remote(
            self.piece(other), self.place(other), self.sems.at[0], self.sems.at[1], {"section": 1 - self.y}
        )

    def begin(self):
        @pl.when(self.y == self.owner)
        def _():
            self.keep().start()

        @pl.when(self.y != self.owner)
        def _():
            self.send().start()

    def finish(self):
        @pl.when(self.y == self.owner)
        def _():
            self.keep().wait()
            self.send().wait_recv()

        @pl.when(self.y != self.owner)
        def _():
            self.send().wait_send()


def end_kernel(
    nf, nd,
    in_ref, in_part1_ref, out_part0_ref, out_part1_ref, small_ref,
    in_all, out_all, small_all,
    in_own, in_landed, in_chain, in_sems, in_part,
    in_final, out_final, small_slots, small_total, local_sem, swap_sem, back_sem, small_sems, group_send, group_recv,
):
    y, z, d = lax.axis_index("section"), lax.axis_index("fsdp"), lax.axis_index("dp")
    away = z != d
    twin = {"fsdp": d, "dp": z}
    peer = {"section": 1 - y}
    lines = small_ref.shape[1]
    wide = lambda k: {"fsdp": (z + k) % nf}
    greet(
        [(None, peer), (away, twin)]
        + [(None, wide(k)) for k in range(1, nf)]
        + [(None, {"dp": flip(d, bit)}) for bit in bits_of(nd)]
    )
    in_sum = SectionSum(in_view(in_ref, nf), nf, y, z, in_own, in_landed, in_chain, in_sems, in_part)
    in_sum.begin()
    small_over = remote(small_ref.at[1 - y], small_slots.at[nf], small_sems.at[0, 0], small_sems.at[1, 0], peer)
    small_over.start()
    small_load = pltpu.make_async_copy(small_ref.at[y], small_slots.at[0], local_sem.at[0])
    small_load.start()
    width = in_final.shape[0]
    part_rows, second = in_parts(width)
    overlap = part_rows - second
    out_rows, out_columns = out_part0_ref.shape
    in_piece = lambda ref: lambda p: ref if p == 0 else ref.at[pl.ds(overlap, width - part_rows)]
    in_place = lambda p: in_final.at[pl.ds(p * part_rows, width - part_rows if p else part_rows)]
    out_place = lambda p: out_final.at[:, pl.ds(p * out_columns, out_columns)]
    out_returns = [
        SectionReturn(lambda p: out_part0_ref, out_place, 0, y, back_sem.at[0]),
        SectionReturn(lambda p: out_part1_ref, out_place, 1, y, back_sem.at[1]),
    ]
    in_returns = [
        SectionReturn(in_piece(in_part), in_place, 0, y, back_sem.at[2]),
        SectionReturn(in_piece(in_part1_ref), in_place, 1, y, back_sem.at[3]),
    ]
    in_groups = [
        GroupRows(
            lambda device, p=p: in_all.at[device, pl.ds(p * part_rows, width - part_rows if p else part_rows)],
            d, nd, group_send.at[p], group_recv.at[p],
        )
        for p in range(2)
    ]
    out_group = GroupRows(rows_of(out_all, out_rows), d, nd, group_send.at[2], group_recv.at[2])
    small_group = GroupRows(rows_of(small_all, lines), d, nd, group_send.at[3], group_recv.at[3])

    small_load.wait()
    small_over.wait()
    small_slots[0] = small_slots[0] + small_slots[nf]
    small_copies = [
        remote(small_slots.at[0], small_slots.at[k], small_sems.at[0, k], small_sems.at[1, k], wide(k))
        for k in range(1, nf)
    ]
    for copy in small_copies:
        copy.start()
    for copy in small_copies:
        copy.wait()
    total = small_slots[0]
    for k in range(1, nf):
        total = total + small_slots[k]
    small_total[...] = total
    small_own = pltpu.make_async_copy(small_total, small_group.part(0), local_sem.at[0])
    small_own.start()
    small_group.begin(small_total)

    swap_target = out_all.at[pl.ds(pl.multiple_of(z * out_rows, 16), out_rows)]
    swap = remote(out_final, swap_target, swap_sem.at[0], swap_sem.at[1], twin)
    stay = pltpu.make_async_copy(out_final, out_group.part(0), swap_sem.at[2])
    for k in range(nf - 1, 0, -1):
        in_sum.stage(k)
        if k == nf - 1:
            for back in out_returns:
                back.begin()
            small_group.finish()
            small_own.wait()
        if k == nf - 2:
            for back in out_returns:
                back.finish()

            @pl.when(away)
            def _():
                swap.start()

            @pl.when(jnp.logical_not(away))
            def _():
                stay.start()

        if k == 1:
            in_returns[1].begin()

            @pl.when(away)
            def _():
                swap.wait()

            @pl.when(jnp.logical_not(away))
            def _():
                stay.wait()

            out_group.begin()
    in_returns[1].finish()
    out_group.finish()
    in_sum.finish()
    in_returns[0].begin()

    @pl.when(y == 0)
    def _():
        in_returns[0].keep().wait()

    def own_copy(p):
        return pltpu.make_async_copy(in_place(p), in_groups[p].part(0), local_sem.at[1 + p])

    own_copy(0).start()
    in_groups[0].begin(in_place(0))

    @pl.when(y == 0)
    def _():
        in_returns[0].send().wait_recv()

    own_copy(1).start()
    in_groups[1].begin(in_place(1))
    in_groups[0].finish()
    in_groups[1].finish()
    own_copy(0).wait()
    own_copy(1).wait()

    @pl.when(y == 1)
    def _():
        in_returns[0].send().wait_send()

    in_sum.settle()


def run_end(nf, nd, in_grad, in_part1, out_part0, out_part1, small):
    anywhere = pl.BlockSpec(memory_space=pl.ANY)
    dma = pltpu.SemaphoreType.DMA
    lines = small.shape[1]
    width = in_grad.shape[-2]
    out_rows = out_part0.shape[0]
    return pl.pallas_call(
        functools.partial(end_kernel, nf, nd),
        in_specs=[anywhere] * 5,
        out_specs=[anywhere] * 3,
        out_shape=[
            jax.ShapeDtypeStruct((nd, width, in_part1.shape[1]), BF16),
            jax.ShapeDtypeStruct((nd * out_rows, D), BF16),
            jax.ShapeDtypeStruct((nd * lines, LANES), F32),
        ],
        scratch_shapes=section_sum_scratch(nf, in_part1.shape)
        + [
            pltpu.VMEM((width, in_part1.shape[1]), BF16),
            pltpu.VMEM((out_rows, D), BF16),
            pltpu.VMEM((nf + 1, lines, LANES), F32),
            pltpu.VMEM((lines, LANES), F32),
            dma((3,)),
            dma((3,)),
            dma((4, 3)),
            dma((2, nf)),
            dma((4, nd)),
            dma((4, nd)),
        ],
        compiler_params=pltpu.CompilerParams(
            vmem_limit_bytes=VMEM_LIMIT, collective_id=6, has_side_effects=True
        ),
        name="sum_end",
    )(in_grad, in_part1, out_part0, out_part1, small)


class Weights:

    def __init__(self, source, held, sems):
        self.source, self.held, self.sems = source, held, sems
        self.blocks = source.shape[0]
        self.columns = source.shape[2]

    def copies(self):
        out = []
        for k in range(self.blocks):
            if len(self.held.shape) == 3:
                target = self.held.at[k]
            else:
                target = self.held.at[:, pl.ds(k * self.columns, self.columns)]
            out.append(pltpu.make_async_copy(self.source.at[k], target, self.sems.at[k]))
        return out

    def forward(self, rows):
        if len(self.held.shape) == 2:
            return dot(rows, self.held[...], ((1,), (1,)))
        total = 0.0
        for k in range(self.blocks):
            total = total + dot(
                rows[:, k * self.columns : (k + 1) * self.columns], self.held[k], ((1,), (1,))
            )
        return total

    def backward(self, rows):
        if len(self.held.shape) == 2:
            return dot(rows, self.held[...])
        return jnp.concatenate([dot(rows, self.held[k]) for k in range(self.blocks)], axis=1)


def held_shape(w_in):
    blocks, width, columns = w_in.shape
    return (width, blocks * columns) if columns % LANES == 0 else (blocks, width, columns)


def own_steps(steps, turn):
    padded = jnp.concatenate([steps, jnp.zeros((steps.shape[0], LANES - H), F32)], axis=1)
    return pltpu.roll(padded, LANES - turn, 1)


def mix_forward(
    ch, proj_ref, meta_ref, segrow_ref, conv_w_ref, conv_b_ref, dtb_ref, alog_ref, skip_ref, gain_ref,
    gated_ref, square_ref, mixed_ref, pre_ref, state_out_ref, pad, state, sub, chunk, turn,
):
    conv_width = ch + 2 * N
    rows = pl.ds(pl.multiple_of(sub * Q, Q), Q)
    meta = meta_ref[rows, :]
    pad[8:, :] = proj_ref[rows, ch : ch + conv_width]
    pre = conv_b_ref[...] + conv_w_ref[3:4, :] * pad[8:, :]
    for lag in range(1, K):
        pre = pre + (conv_w_ref[3 - lag : 4 - lag, :] * meta[:, lag : lag + 1]) * pad[8 - lag : 8 - lag + Q, :]
    pad[0:8, :] = pad[Q : Q + 8, :]
    pre_ref[rows, :] = pre
    conv_out = pre * jax.nn.sigmoid(pre)
    values = conv_out[:, :ch]
    b_part = conv_out[:, ch : ch + N]
    c_part = conv_out[:, ch + N :]
    row, column = triangles()
    tri = jnp.where(row >= column, 1.0, 0.0)
    shifted, step, log_decay, cumulative = decay_tables(
        own_steps(proj_ref[rows, ch + conv_width :], turn), dtb_ref[...], alog_ref[...], tri
    )
    linked = (row >= column) & (meta[:, 0:1] == segrow_ref[sub])
    inner = jnp.where(linked, low_dot(c_part, b_part, ((1,), (1,))), 0.0)
    cum_t = cumulative.T
    step_t = step.T
    last = cumulative[Q - 1 : Q, :]
    entry = meta[:, 4:5] * jnp.exp(cumulative)
    weight = meta[:, 5:6] * jnp.exp(last - cumulative) * step
    state_in = state[...]
    state_out_ref[sub] = state_in
    carried = low_dot(c_part, state_in)
    low_half = lax.broadcasted_iota(jnp.int32, (Q, LANES), 1) < P_SIZE
    squares = jnp.zeros((Q, 1), F32)
    weighted = []
    entries = []
    for pair in range(ch // LANES):
        lanes = slice(pair * LANES, (pair + 1) * LANES)
        values_pair = values[:, lanes]
        mats = []
        for head in (2 * pair, 2 * pair + 1):
            spread = jnp.minimum(cumulative[:, head : head + 1] - cum_t[head : head + 1, :], 0.0)
            mats.append((inner * jnp.exp(spread) * step_t[head : head + 1, :]).astype(BF16))
        zero = jnp.zeros_like(values_pair)
        stacked = jnp.concatenate(
            [jnp.where(low_half, values_pair, zero), jnp.where(low_half, zero, values_pair)], axis=0
        ).astype(BF16)
        out = dot(jnp.concatenate(mats, axis=1), stacked)
        entry_pair = pair_lanes(entry, 2 * pair, low_half)
        out = out + entry_pair * carried[:, lanes] + skip_ref[:, lanes] * values_pair
        mixed_ref[rows, lanes] = out
        gate = proj_ref[rows, lanes]
        gated = out * (gate * jax.nn.sigmoid(gate))
        squares = squares + jnp.sum(gated * gated, axis=1, keepdims=True)
        gated_ref[rows, lanes] = (gated * gain_ref[:, lanes]).astype(BF16)
        weighted.append((pair_lanes(weight, 2 * pair, low_half) * values_pair).astype(BF16))
        entries.append(entry_pair[Q - 1 : Q, :])
    square_ref[0, pl.ds(chunk, 1), :] = to_row(squares)
    state[...] = jnp.concatenate(entries, axis=1) * state_in + dot(
        b_part.T.astype(BF16), jnp.concatenate(weighted, axis=1)
    )


def layer_kernel(
    ch, rows, nf, nd, final,
    normed_ref, meta_ref, segrow_ref, conv_w_ref, conv_b_ref, dtb_ref, alog_ref, skip_ref, gain_ref,
    w_in_ref, w_out_ref, hidden_ref, extra_ref, *refs,
):
    if not final:
        cot_ref, out_ref, _ = refs[:3]
        refs = refs[3:]
    (
        proj_ref, gated_ref, mixed_ref, pre_ref, state_out_ref, branch_ref, next_ref, ratio_ref, pull_ref, moved_ref,
        *refs,
    ) = refs
    if final:
        cot_all, refs = refs[0], refs[1:]
    else:
        w_in1, w_out1, cot_own = refs[:3]
        in_sems, out_sems = refs[-2:]
        refs = refs[3:-2]
    (
        held, w_out, pad, state, partial, landed, squares, pulls, low,
        sum_send, sum_recv, tile_send, tile_recv, group_send, group_recv, local_sem, load_sem, cot_sem,
    ) = refs
    step = pl.program_id(0)
    y, z, d = lax.axis_index("section"), lax.axis_index("fsdp"), lax.axis_index("dp")
    block = normed_ref.shape[0]
    subs = block // Q
    steps = pl.num_programs(0)
    pieces = partial.shape[0] // Q
    step_count = pieces // subs
    per_rank = rows // Q
    bits = bits_of(nd)
    away = z != d
    twin = {"fsdp": d, "dp": z}
    group = GroupSum(partial, landed, per_rank, d, nd, sum_send, sum_recv)
    weights = Weights(w_in_ref, held, load_sem)
    out_load = pltpu.make_async_copy(w_out_ref, w_out, local_sem.at[3])
    if final:
        cot_group = GroupRows(rows_of(cot_all, rows), d, nd, cot_sem.at[0], cot_sem.at[1])
        cot_keep = pltpu.make_async_copy(extra_ref, cot_group.part(0), local_sem.at[4])
    else:
        gather = SectionGather(w_in1, 1, nf, y, z, in_sems)
        outs = OutGather(out_ref, w_out1, 1, nf, y, z, d, out_sems)
        cot_swap = remote(cot_ref.at[y], cot_own, cot_sem.at[0, 0], cot_sem.at[1, 0], twin)
        cot_stay = pltpu.make_async_copy(cot_ref.at[y], cot_own, cot_sem.at[0, 0])

    @pl.when(step == 0)
    def _():
        for copy in weights.copies():
            copy.start()
        out_load.start()
        greet(
            [(None, {"dp": flip(d, j)}) for j in range(1, nd)]
            + [(away, twin)]
            + ([] if final else line_neighbours(nf, y, z))
        )
        if final:
            cot_keep.start()
            cot_group.begin(extra_ref)
        else:
            gather.relay(1)
            outs.begin()

            @pl.when(away)
            def _():
                cot_swap.start()

            @pl.when(jnp.logical_not(away))
            def _():
                cot_stay.start()

        pad[0:8, :] = jnp.zeros((8, pad.shape[1]), F32)
        state[...] = jnp.zeros_like(state)
        for copy in weights.copies():
            copy.wait()
        out_load.wait()

    proj_ref[...] = weights.forward(normed_ref[...])

    def one_chunk(sub, carry):
        mix_forward(
            ch, proj_ref, meta_ref, segrow_ref, conv_w_ref, conv_b_ref, dtb_ref, alog_ref, skip_ref, gain_ref,
            gated_ref, squares, mixed_ref, pre_ref, state_out_ref, pad, state, sub, step * subs + sub, d * (H // nd),
        )
        return carry

    lax.fori_loop(0, subs, one_chunk, 0)
    here_rows = pl.ds(pl.multiple_of(step * block, block), block)
    partial[here_rows, :] = dot(gated_ref[...], w_out[...]).astype(BF16)

    for k in range(len(bits)):

        @pl.when(step >= k)
        def _():
            for sub in range(subs):
                group.send(k, (step - k) * subs + sub)

    if final:

        @pl.when(step == min(2, step_count - 1))
        def _():
            cot_group.finish()

    else:
        for k in range(1, nf):

            @pl.when(step == min(k, step_count - 1))
            def _():
                if k == 1:
                    outs.begin_other()
                else:
                    gather.arrive(k)
                    gather.relay(k)
                outs.hops(k)

    @pl.when(step == steps - 1)
    def _():
        for k in range(1, len(bits)):
            for late in range(k):
                for sub in range(subs):
                    group.send(k, pieces - (late + 1) * subs + sub)
        total = group_tiles(squares, tile_send, tile_recv, d, nd)
        ratio = lax.rsqrt(total * (1.0 / DI) + EPSILON)
        ratio_ref[...] = ratio
        pulls[0] = jnp.zeros(pulls.shape[1:], F32)
        for part in range(per_rank):
            piece = d * per_rank + part
            here = slice(part * Q, (part + 1) * Q)
            branch = group.own(piece) * to_column(ratio_ref[pl.ds(piece, 1), :])
            branch_ref[here, :] = branch
            moved = (hidden_ref[here, :].astype(F32) + branch).astype(BF16)
            next_ref[here, :] = moved
            if final:
                low[here, :] = moved
                pulls[0, pl.ds(piece, 1), :] = to_row(
                    jnp.sum(extra_ref[here, :].astype(F32) * branch, axis=1, keepdims=True)
                )
            else:
                values = moved.astype(F32)
                low[here, :] = (values * rms_parts(values) * extra_ref[...]).astype(BF16)
        if final:
            swap = remote(low, moved_ref, local_sem.at[0], local_sem.at[1], twin)
            stay = pltpu.make_async_copy(low, moved_ref, local_sem.at[2])

            @pl.when(away)
            def _():
                swap.start()

            @pl.when(jnp.logical_not(away))
            def _():
                stay.start()

            pull_ref[...] = group_tiles(pulls, group_send, group_recv, d, nd)

            @pl.when(away)
            def _():
                swap.wait()

            @pl.when(jnp.logical_not(away))
            def _():
                stay.wait()
        else:
            pull_ref[...] = jnp.zeros_like(pull_ref)
            every = GroupRows(rows_of(moved_ref, rows), d, nd, group_send, group_recv)
            mine = pltpu.make_async_copy(low, every.part(0), local_sem.at[0])
            mine.start()
            every.begin(low)
            every.finish()
            mine.wait()

            for k in range(1, nf):
                gather.settle(k)
            outs.settle()

            @pl.when(away)
            def _():
                cot_swap.wait()

            @pl.when(jnp.logical_not(away))
            def _():
                cot_stay.wait()

        if final:
            cot_keep.wait()
        group.settle(pieces)


def once(shape):
    return pl.BlockSpec(shape, lambda s: (0,) * len(shape), pipeline_mode=pl.Buffered(buffer_count=1))


def pick(part, layer):
    return pl.BlockSpec(
        (None,) + part.shape[1:], lambda s: (layer, 0, 0), pipeline_mode=pl.Buffered(buffer_count=1)
    )


def run_layer(
    ch, rows, nf, nd, final, normed_all, meta, segrow, small, w_in, w_out, hidden, extra, identity, *more
):
    length, width = normed_all.shape[0], w_in.shape[1]
    layer = 1 if final else 0
    conv_width = ch + 2 * N
    block = 2 * Q
    steps = length // block
    pieces = length // Q
    subs = block // Q
    bits = len(bits_of(nd))
    dma = pltpu.SemaphoreType.DMA
    anywhere = pl.BlockSpec(memory_space=pl.ANY)
    ordered = lambda s: (s, 0)
    ordered3 = lambda s: (s, 0, 0)
    return pl.pallas_call(
        functools.partial(layer_kernel, ch, rows, nf, nd, final),
        grid=(steps,),
        in_specs=[
            pl.BlockSpec((block, D), ordered),
            pl.BlockSpec((block, LANES), ordered),
            pl.BlockSpec((subs, 1, Q), ordered3),
        ]
        + [pick(part, layer) for part in small]
        + [
            anywhere,
            anywhere,
            once((rows, D)),
            once((rows, D)) if final else pick(extra, 1),
        ]
        + [anywhere] * len(more),
        out_specs=[
            pl.BlockSpec((block, width), ordered),
            pl.BlockSpec((block, ch), ordered),
            pl.BlockSpec((block, ch), ordered),
            pl.BlockSpec((block, conv_width), ordered),
            pl.BlockSpec((subs, N, ch), ordered3),
            once((rows, D)),
            once((rows, D)),
            once((pieces, Q)),
            once((pieces, Q)),
            anywhere,
        ]
        + [anywhere] * (1 if final else 3),
        out_shape=[
            jax.ShapeDtypeStruct((length, width), F32),
            jax.ShapeDtypeStruct((length, ch), BF16),
            jax.ShapeDtypeStruct((length, ch), F32),
            jax.ShapeDtypeStruct((length, conv_width), F32),
            jax.ShapeDtypeStruct((pieces, N, ch), F32),
            jax.ShapeDtypeStruct((rows, D), F32),
            jax.ShapeDtypeStruct((rows, D), BF16),
            jax.ShapeDtypeStruct((pieces, Q), F32),
            jax.ShapeDtypeStruct((pieces, Q), F32),
            jax.ShapeDtypeStruct((rows if final else length, D), BF16),
        ]
        + (
            [jax.ShapeDtypeStruct((length, D), BF16)]
            if final
            else [
                jax.ShapeDtypeStruct(w_in.shape, BF16),
                jax.ShapeDtypeStruct((ch, D), BF16),
                jax.ShapeDtypeStruct((rows, D), BF16),
            ]
        ),
        scratch_shapes=[
            pltpu.VMEM(held_shape(w_in), BF16),
            pltpu.VMEM((ch, D), BF16),
            pltpu.VMEM((Q + 8, conv_width), F32),
            pltpu.VMEM((N, ch), F32),
            pltpu.VMEM((length, D), BF16),
            pltpu.VMEM((bits, length, D), BF16),
            pltpu.VMEM((nd, pieces, Q), F32),
            pltpu.VMEM((nd, pieces, Q), F32),
            pltpu.VMEM((rows, D), BF16),
            dma((bits, pieces)),
            dma((bits, pieces)),
            dma((nd,)),
            dma((nd,)),
            dma((nd,)),
            dma((nd,)),
            dma((5,)),
            dma((nf,)),
            dma((2, nd)),
        ]
        + ([] if final else [dma((7, 2 * nf)), dma((6, 4))]),
        input_output_aliases={} if final else {15: 10},
        compiler_params=pltpu.CompilerParams(
            vmem_limit_bytes=VMEM_LIMIT, collective_id=identity, has_side_effects=True
        ),
        name="layer_last" if final else "layer_first",
    )(normed_all, meta, segrow, *small, w_in, w_out, hidden, extra, *more)


def mix_backward(
    ch, proj_ref, pre_ref, mixed_ref, state_ref, grad_ref, ratio_ref, pull_ref, meta_ref, segrow_ref,
    conv_w_ref, dtb_ref, alog_ref, skip_ref, gain_ref,
    dproj_ref, dconv_w_ref, dchan_ref, ddecay_ref, tail, dstate, sub, chunk, turn,
):
    conv_width = ch + 2 * N
    rows = pl.ds(pl.multiple_of(sub * Q, Q), Q)
    meta = meta_ref[rows, :]
    pre = pre_ref[rows, :]
    sig = jax.nn.sigmoid(pre)
    conv_out = pre * sig
    values = conv_out[:, :ch]
    b_part = conv_out[:, ch : ch + N]
    c_part = conv_out[:, ch + N :]
    row, column = triangles()
    tri = jnp.where(row >= column, 1.0, 0.0)
    shifted, step, log_decay, cumulative = decay_tables(
        own_steps(proj_ref[rows, ch + conv_width :], turn), dtb_ref[...], alog_ref[...], tri
    )
    linked = (row <= column) & (meta[:, 0:1] == segrow_ref[sub])
    b_low = b_part.astype(BF16)
    c_low = c_part.astype(BF16)
    inner = jnp.where(linked, dot(b_low, c_low, ((1,), (1,))), 0.0)
    cum_t = cumulative.T
    last = cumulative[Q - 1 : Q, :]
    entry = meta[:, 4:5] * jnp.exp(cumulative)
    weight = meta[:, 5:6] * jnp.exp(last - cumulative)
    state_in = state_ref[sub]
    dstate_in = dstate[...]
    state_low = state_in.astype(BF16)
    dstate_low = dstate_in.astype(BF16)
    carried = dot(c_low, state_low)
    carried_back = dot(b_low, dstate_low)
    low_half = lax.broadcasted_iota(jnp.int32, (Q, LANES), 1) < P_SIZE
    lane = lax.broadcasted_iota(jnp.int32, (Q, LANES), 1)
    ratio = to_column(ratio_ref[pl.ds(chunk, 1), :])
    pull = ratio * ratio * to_column(pull_ref[pl.ds(chunk, 1), :]) * (1.0 / DI)
    dinner = jnp.zeros((Q, Q), F32)
    dcum = jnp.zeros((Q, LANES), F32)
    dcum_rows = []
    dexit = jnp.zeros((Q, LANES), F32)
    dstep = jnp.zeros((Q, LANES), F32)
    dcum_entry = jnp.zeros((Q, LANES), F32)
    weighted = []
    entered = []
    entry_rows = []
    dpre_parts = []
    for pair in range(ch // LANES):
        lanes = slice(pair * LANES, (pair + 1) * LANES)
        values_pair = values[:, lanes]
        gate = proj_ref[rows, lanes]
        mixed = mixed_ref[rows, lanes]
        gate_sig = jax.nn.sigmoid(gate)
        gate_silu = gate * gate_sig
        gated = mixed * gate_silu
        scaled = grad_ref[rows, lanes] * ratio
        dchan_ref[0:1, lanes] += jnp.sum(scaled * gated, axis=0, keepdims=True)
        dgated = scaled * gain_ref[:, lanes] - gated * pull
        dproj_ref[rows, lanes] = (dgated * mixed * (gate_sig + gate_silu * (1.0 - gate_sig))).astype(BF16)
        dmixed = dgated * gate_silu
        dchan_ref[1:2, lanes] += jnp.sum(dmixed * values_pair, axis=0, keepdims=True)
        zero = jnp.zeros_like(values_pair)
        dmixed_halves = [jnp.where(low_half, dmixed, zero).astype(BF16), jnp.where(low_half, zero, dmixed).astype(BF16)]
        values_low = values_pair.astype(BF16)
        step_pair = pair_lanes(step, 2 * pair, low_half)
        mats = []
        for half, head in enumerate((2 * pair, 2 * pair + 1)):
            spread = jnp.minimum(cum_t[head : head + 1, :] - cumulative[:, head : head + 1], 0.0)
            plain = jnp.exp(spread)
            decay = plain * step[:, head : head + 1]
            product = dot(values_low, dmixed_halves[half], ((1,), (1,)))
            mats.append((inner * plain).astype(BF16))
            spreaded = product * decay
            dinner = dinner + spreaded
            turned = spreaded * inner
            dcum = dcum - jnp.where(lane == head, jnp.sum(turned, axis=1, keepdims=True), 0.0)
            dcum_rows.append(jnp.sum(turned, axis=0, keepdims=True))
        back = dot(jnp.concatenate(mats, axis=1), jnp.concatenate(dmixed_halves, axis=0))
        weight_pair = pair_lanes(weight, 2 * pair, low_half)
        through = weight_pair * carried_back[:, lanes]
        total = back + through
        dvalues = step_pair * total + skip_ref[:, lanes] * dmixed
        step_terms = total * values_pair
        exit_terms = through * values_pair * step_pair
        entry_pair = pair_lanes(entry, 2 * pair, low_half)
        entry_grad = entry_pair * dmixed
        entry_terms = entry_grad * carried[:, lanes]
        for half, head in enumerate((2 * pair, 2 * pair + 1)):
            own = lane == head
            mask = low_half if half == 0 else ~low_half
            dstep = dstep + jnp.where(own, jnp.sum(jnp.where(mask, step_terms, 0.0), axis=1, keepdims=True), 0.0)
            dexit = dexit + jnp.where(own, jnp.sum(jnp.where(mask, exit_terms, 0.0), axis=1, keepdims=True), 0.0)
            dcum_entry = dcum_entry + jnp.where(own, jnp.sum(jnp.where(mask, entry_terms, 0.0), axis=1, keepdims=True), 0.0)
        weighted.append((weight_pair * step_pair * values_pair).astype(BF16))
        entered.append(entry_grad.astype(BF16))
        entry_rows.append(entry_pair[Q - 1 : Q, :])
        dpre_parts.append(dvalues)
    weighted = jnp.concatenate(weighted, axis=1)
    entered = jnp.concatenate(entered, axis=1)
    entry_rows = jnp.concatenate(entry_rows, axis=1)
    dinner_low = jnp.where(linked, dinner, 0.0).astype(BF16)
    db = dot(dinner_low, c_low) + dot(weighted, dstate_low, ((1,), (1,)))
    dc = dot(dinner_low.T, b_low) + dot(entered, state_low, ((1,), (1,)))
    state_terms = jnp.sum(state_in * dstate_in, axis=0, keepdims=True) * entry_rows
    head_lane = lax.broadcasted_iota(jnp.int32, (1, LANES), 1)
    state_sum = jnp.zeros((1, LANES), F32)
    for head in range(ch // P_SIZE):
        part = jnp.sum(state_terms[:, head * P_SIZE : (head + 1) * P_SIZE], axis=1, keepdims=True)
        state_sum = state_sum + jnp.where(head_lane == head, part, 0.0)
    by_row = jnp.concatenate(dcum_rows + [jnp.zeros((LANES - len(dcum_rows), Q), F32)], axis=0)
    dcum = dcum + by_row.T + dcum_entry
    later = jnp.where(row <= column, 1.0, 0.0)
    before = jnp.where(row > column, 1.0, 0.0)
    dlog = fine_dot(later, dcum) + fine_dot(before, dexit) + state_sum
    growth = jnp.exp(alog_ref[...])
    dstep = dstep - dlog * growth
    ddt = dstep * jax.nn.sigmoid(shifted)
    ddecay_ref[0:1, :] += jnp.sum(ddt, axis=0, keepdims=True)
    ddecay_ref[1:2, :] += jnp.sum(dlog * log_decay, axis=0, keepdims=True)
    heads = ch // P_SIZE
    dproj_ref[rows, ch + conv_width :] = pltpu.roll(jnp.where(lane < heads, ddt, 0.0), turn, 1)[:, :H].astype(BF16)
    dstate[...] = entry_rows * dstate_in + dot(c_part.T.astype(BF16), entered)
    dconv_out = jnp.concatenate(dpre_parts + [db, dc], axis=1)
    dpre = dconv_out * (sig + conv_out * (1.0 - sig))
    raw = proj_ref[rows, ch : ch + conv_width]
    dchan_ref[2:3, :] += jnp.sum(dpre, axis=0, keepdims=True)
    draw = conv_w_ref[3:4, :] * dpre
    dconv_w_ref[3:4, :] += jnp.sum(raw * dpre, axis=0, keepdims=True)
    for lag in range(1, K):
        kept = meta[:, lag : lag + 1] * dpre
        tail[lag - 1, 0:Q, :] = kept
        moved = tail[lag - 1, lag : lag + Q, :]
        tail[lag - 1, Q : Q + 8, :] = kept[0:8, :]
        draw = draw + conv_w_ref[3 - lag : 4 - lag, :] * moved
        dconv_w_ref[3 - lag : 4 - lag, :] += jnp.sum(raw * moved, axis=0, keepdims=True)
    dproj_ref[rows, ch : ch + conv_width] = draw.astype(BF16)


def layer_back_kernel(
    ch, rows, nf, nd, last,
    grad_all_ref, proj_ref, pre_ref, mixed_ref, state_ref, meta_ref, segrow_ref, ratio_ref, pull_ref,
    conv_w_ref, dtb_ref, alog_ref, skip_ref, gain_ref, w_in_ref, w_out_ref,
    hidden_ref, grad_own_ref, norm_gain_ref, branch_ref, *refs,
):
    count = 2 if last else 1
    sources, refs = refs[:count], refs[count:]
    (
        dproj_ref, dconv_w_ref, dchan_ref, ddecay_ref, dgain_ref, next_ref, next_pull_ref, moved_ref,
    ) = refs[:8]
    results, refs = refs[8 : 8 + count], refs[8 + count :]
    (
        held, w_out, tail, dstate, dnout, partial, landed, pulls, low,
        sum_send, sum_recv, tile_send, tile_recv, group_send, group_recv, local_sem, load_sem,
    ) = refs[:17]
    refs = refs[17:]
    step = pl.program_id(0)
    y, z, d = lax.axis_index("section"), lax.axis_index("fsdp"), lax.axis_index("dp")
    block = grad_all_ref.shape[0]
    subs = block // Q
    steps = pl.num_programs(0)
    pieces = partial.shape[0] // Q
    per_rank = rows // Q
    bits = bits_of(nd)
    away = z != d
    twin = {"fsdp": d, "dp": z}
    group = GroupSum(partial, landed, per_rank, d, nd, sum_send, sum_recv)
    place = steps - 1 - step
    step_count = pieces // subs
    sums = [
        SectionSum(make(source, nf), nf, y, z, *refs[5 * k : 5 * k + 5])
        for k, (make, source) in enumerate(zip((out_view, in_view), sources))
    ]
    weights = Weights(w_in_ref, held, load_sem)
    out_load = pltpu.make_async_copy(w_out_ref, w_out, local_sem.at[3])

    @pl.when(step == 0)
    def _():
        for copy in weights.copies():
            copy.start()
        out_load.start()
        greet(
            [(None, {"dp": flip(d, j)}) for j in range(1, nd)]
            + line_neighbours(nf, y, z)
            + ([(away, twin)] if last else [])
        )
        for one in sums:
            one.begin()
        tail[...] = jnp.zeros_like(tail)
        dstate[...] = jnp.zeros_like(dstate)
        dconv_w_ref[...] = jnp.zeros_like(dconv_w_ref)
        dchan_ref[...] = jnp.zeros_like(dchan_ref)
        ddecay_ref[...] = jnp.zeros_like(ddecay_ref)
        for copy in weights.copies():
            copy.wait()
        out_load.wait()

    dnout[...] = dot(grad_all_ref[...], w_out[...], ((1,), (1,)))

    def one_chunk(turn, carry):
        sub = subs - 1 - turn
        mix_backward(
            ch, proj_ref, pre_ref, mixed_ref, state_ref, dnout, ratio_ref, pull_ref, meta_ref, segrow_ref,
            conv_w_ref, dtb_ref, alog_ref, skip_ref, gain_ref,
            dproj_ref, dconv_w_ref, dchan_ref, ddecay_ref, tail, dstate, sub, place * subs + sub, d * (H // nd),
        )
        return carry

    lax.fori_loop(0, subs, one_chunk, 0)
    partial[pl.ds(pl.multiple_of(place * block, block), block), :] = weights.backward(
        dproj_ref[...]
    ).astype(BF16)

    for k in range(len(bits)):

        @pl.when(step >= k)
        def _():
            for sub in range(subs):
                group.send(k, (place + k) * subs + sub)

    for k in range(nf - 1, 0, -1):

        @pl.when(step == min(nf - 1 - k, step_count - 1))
        def _():
            for one in sums:
                one.stage(k)

    @pl.when(step == steps - 1)
    def _():
        for k in range(1, len(bits)):
            for late in range(k):
                for sub in range(subs):
                    group.send(k, late * subs + sub)
        pulls[0] = jnp.zeros(pulls.shape[1:], F32)
        dgain = jnp.zeros((1, D), F32)
        for part in range(per_rank):
            piece = d * per_rank + part
            here = slice(part * Q, (part + 1) * Q)
            dnormed = group.own(piece)
            hidden = hidden_ref[here, :].astype(F32)
            inverse = rms_parts(hidden)
            dgain = dgain + jnp.sum(dnormed * hidden * inverse, axis=0, keepdims=True)
            scaled = dnormed * norm_gain_ref[...]
            dhidden = inverse * (
                scaled - hidden * (inverse * inverse) * jnp.mean(scaled * hidden, axis=1, keepdims=True)
            )
            moved = (grad_own_ref[here, :].astype(F32) + dhidden).astype(BF16)
            low[here, :] = moved
            next_ref[here, :] = moved
            if not last:
                pulls[0, pl.ds(piece, 1), :] = to_row(
                    jnp.sum(moved.astype(F32) * branch_ref[here, :], axis=1, keepdims=True)
                )
        dgain_ref[...] = dgain
        if last:
            swap = remote(low, moved_ref, local_sem.at[0], local_sem.at[1], twin)
            stay = pltpu.make_async_copy(low, moved_ref, local_sem.at[2])

            @pl.when(away)
            def _():
                swap.start()
                swap.wait()

            @pl.when(jnp.logical_not(away))
            def _():
                stay.start()
                stay.wait()

            next_pull_ref[...] = jnp.zeros_like(next_pull_ref)
        else:
            every = GroupRows(rows_of(moved_ref, rows), d, nd, group_send, group_recv)
            mine = pltpu.make_async_copy(low, every.part(0), local_sem.at[0])
            mine.start()
            every.begin(low)
            next_pull_ref[...] = group_tiles(pulls, tile_send, tile_recv, d, nd)
            every.finish()
            mine.wait()
        group.settle(pieces)
        for one, result in zip(sums, results):
            one.finish()
            copy = pltpu.make_async_copy(one.result, result, local_sem.at[1])
            copy.start()
            copy.wait()
            one.settle()


def run_layer_back(
    ch, rows, nf, nd, last, grad_all, proj, pre, mixed, states, meta, segrow, ratio, pull, small, w_in, w_out,
    hidden, grad_own, norm_gain, branch, identity, *sums,
):
    length, width = proj.shape
    shapes = [make(nf, g) for make, g in zip((out_part_shape, in_part_shape), sums)]
    conv_width = ch + 2 * N
    block = 2 * Q
    steps = length // block
    pieces = length // Q
    subs = block // Q
    bits = len(bits_of(nd))
    dma = pltpu.SemaphoreType.DMA
    ordered = lambda s: (steps - 1 - s, 0)
    ordered3 = lambda s: (steps - 1 - s, 0, 0)
    layer = 0 if last else 1
    conv_w, conv_b, dtb, alog, skip, gain = small
    return pl.pallas_call(
        functools.partial(layer_back_kernel, ch, rows, nf, nd, last),
        grid=(steps,),
        in_specs=[
            pl.BlockSpec((block, D), ordered),
            pl.BlockSpec((block, width), ordered),
            pl.BlockSpec((block, conv_width), ordered),
            pl.BlockSpec((block, ch), ordered),
            pl.BlockSpec((subs, N, ch), ordered3),
            pl.BlockSpec((block, LANES), ordered),
            pl.BlockSpec((subs, 1, Q), ordered3),
            once((pieces, Q)),
            once((pieces, Q)),
        ]
        + [pick(part, layer) for part in (conv_w, dtb, alog, skip, gain)]
        + [
            pl.BlockSpec(memory_space=pl.ANY),
            pl.BlockSpec(memory_space=pl.ANY),
            once((rows, D)),
            once((rows, D)),
            pick(norm_gain, layer),
            once((rows, D)),
        ]
        + [pl.BlockSpec(memory_space=pl.ANY)] * len(sums),
        out_specs=[
            pl.BlockSpec((block, width), ordered),
            once((K, conv_width)),
            once((8, conv_width)),
            once((8, LANES)),
            once((1, D)),
            once((rows, D)),
            once((pieces, Q)),
            pl.BlockSpec(memory_space=pl.ANY),
        ]
        + [pl.BlockSpec(memory_space=pl.ANY)] * len(sums),
        out_shape=[
            jax.ShapeDtypeStruct((length, width), BF16),
            jax.ShapeDtypeStruct((K, conv_width), F32),
            jax.ShapeDtypeStruct((8, conv_width), F32),
            jax.ShapeDtypeStruct((8, LANES), F32),
            jax.ShapeDtypeStruct((1, D), F32),
            jax.ShapeDtypeStruct((rows, D), BF16),
            jax.ShapeDtypeStruct((pieces, Q), F32),
            jax.ShapeDtypeStruct((rows if last else length, D), BF16),
        ]
        + [jax.ShapeDtypeStruct(shape, BF16) for shape in shapes],
        scratch_shapes=[
            pltpu.VMEM(held_shape(w_in), BF16),
            pltpu.VMEM((ch, D), BF16),
            pltpu.VMEM((K - 1, Q + 8, conv_width), F32),
            pltpu.VMEM((N, ch), F32),
            pltpu.VMEM((block, ch), F32),
            pltpu.VMEM((length, D), BF16),
            pltpu.VMEM((bits, length, D), BF16),
            pltpu.VMEM((nd, pieces, Q), F32),
            pltpu.VMEM((rows, D), BF16),
            dma((bits, pieces)),
            dma((bits, pieces)),
            dma((nd,)),
            dma((nd,)),
            dma((nd,)),
            dma((nd,)),
            dma((4,)),
            dma((nf,)),
        ]
        + [part for shape in shapes for part in section_sum_scratch(nf, shape)],
        compiler_params=pltpu.CompilerParams(
            vmem_limit_bytes=VMEM_LIMIT, collective_id=identity, has_side_effects=True
        ),
        name="layer_back_last" if last else "layer_back_first",
    )(
        grad_all, proj, pre, mixed, states, meta, segrow, ratio, pull, conv_w, dtb, alog, skip, gain, w_in, w_out,
        hidden, grad_own, norm_gain, branch, *sums,
    )


def shards(
    inputs, segment, cotangent, norm_gain, in_weight, conv_weight, conv_bias, dt_bias, a_log, d_skip,
    gate_gain, out_weight,
):
    fsdp, dp = lax.axis_size("fsdp"), lax.axis_size("dp")
    section, here = lax.axis_index("section"), lax.axis_index("dp")
    rows = inputs.shape[2]
    ch = DI // dp
    heads = H // dp
    conv_width = ch + 2 * N
    seg_mine = lax.dynamic_index_in_dim(segment, section, 0, keepdims=False)[0].astype(F32)
    seg_mine = jnp.broadcast_to(seg_mine.reshape(rows // Q, 1, Q), (rows // Q, 8, Q)).reshape(-1, Q)
    head_table = jnp.pad(
        jnp.concatenate([dt_bias[0], a_log[0], d_skip[0]], axis=0), ((0, 0), (0, LANES - H))
    )
    hidden, normed_all, w_in0, w_in1, w_out0, seg_all, *table = run_start(
        fsdp, dp, rows, inputs[:, 0], seg_mine, in_weight[0, 0].T, out_weight[0, 0], conv_weight[0, 0], conv_bias[0],
        norm_gain[0], gate_gain[0], head_table,
    )
    *small, gains, meta = table
    length = meta.shape[0]
    segrow = seg_all.reshape(-1, 8, Q)[:, :1]
    saved = []
    for layer in range(2):
        last = layer == 1
        proj, gated, mixed, pre, states, branch, after, ratio, pull, moved, *more = run_layer(
            ch, rows, fsdp, dp, last, normed_all, meta, segrow, small, full_in if last else w_in0,
            full_out if last else w_out0, hidden, cot_own if last else gains, 2 + layer,
            *(() if last else (cotangent[:, 0], out_weight[0, 0], w_in1)),
        )
        saved.append((normed_all, hidden, proj, gated, mixed, pre, states, branch, ratio))
        normed_all, hidden = moved, after
        if last:
            (cot_all,) = more
        else:
            full_in, full_out, cot_own = more
    final = moved

    grad_all, grad_own = cot_all, cot_own
    in_grad, small_grads, parts = (), [None, None], []
    for layer in (1, 0):
        last = layer == 0
        normed_all, hidden, proj, gated, mixed, pre, states, branch, ratio = saved[layer]
        out_grad = dot((gated.astype(F32) * ratio.reshape(length, 1)).astype(BF16), grad_all, ((0,), (0,)))
        dproj, dconv_w, dchan, ddecay, dgain, after, next_pull, moved, *done = run_layer_back(
            ch, rows, fsdp, dp, last, grad_all, proj, pre, mixed, states, meta, segrow, ratio, pull, small,
            w_in0 if last else full_in, w_out0 if last else full_out, hidden, grad_own, gains, saved[0][7], 4 + layer,
            out_grad.astype(BF16), *in_grad,
        )
        parts += done
        grad = dot(dproj, normed_all, ((0,), (0,))).astype(BF16)
        if D // fsdp % LANES:
            grad = jnp.swapaxes(grad.reshape(-1, fsdp, D // fsdp), 0, 1)
        in_grad = (grad,)
        small_grads[layer] = (dgain[0], dconv_w, dchan, ddecay)
        grad_all, grad_own, pull = moved, after, next_pull
    input_grad = moved

    def pack_small(grads):
        dgain, dconv_w, dchan, ddecay = grads
        skip = jnp.sum(dchan[1, :ch].reshape(heads, P_SIZE), axis=1)
        pieces = [dgain, dconv_w.reshape(-1), dchan[2], dchan[0, :ch], ddecay[0, :heads], ddecay[1, :heads], skip]
        flat = jnp.concatenate(pieces)
        return jnp.pad(flat, (0, -flat.shape[0] % 1024)).reshape(-1, LANES)

    packed = jnp.stack([pack_small(grads) for grads in small_grads])
    in_all, out_all, small_sum = run_end(fsdp, dp, in_grad[0], parts[2], parts[1], parts[0], packed)
    in_total = jnp.concatenate(
        [
            in_all[:, :ch].reshape(DI, -1).astype(F32),
            in_all[:, ch : 2 * ch].reshape(DI, -1).astype(F32),
            jnp.sum(in_all[:, 2 * ch :].astype(F32), axis=0),
        ],
        axis=0,
    ).T
    out_total = out_all.astype(F32)
    everything = small_sum.reshape(dp, -1)
    offset = 0
    pieces = []
    for size in (D, K * conv_width, conv_width, ch, heads, heads, heads):
        pieces.append(everything[:, offset : offset + size])
        offset += size
    gain_total = jnp.sum(pieces[0], axis=0)
    convw = pieces[1].reshape(dp, K, conv_width)
    convw_total = jnp.concatenate(
        [jnp.moveaxis(convw[:, :, :ch], 0, 1).reshape(K, DI), jnp.sum(convw[:, :, ch:], axis=0)], axis=1
    )
    convb = pieces[2]
    convb_total = jnp.concatenate([convb[:, :ch].reshape(DI), jnp.sum(convb[:, ch:], axis=0)])
    gate_total = pieces[3].reshape(DI)
    dtb_total, alog_total, skip_total = (piece.reshape(H) for piece in pieces[4:])
    return (
        final[None, None],
        input_grad[None, None],
        gain_total[None, None],
        in_total[None, None],
        convw_total[None, None],
        convb_total[None, None],
        dtb_total[None, None],
        alog_total[None, None],
        skip_total[None, None],
        gate_total[None, None],
        out_total[None, None],
    )


def solution(mesh):
    return jax.shard_map(
        shards,
        mesh=mesh,
        in_specs=(
            P(None, "dp", "fsdp", None),
            P(None, "dp", "fsdp"),
            P(None, "dp", "fsdp", None),
            P("section", None, None),
            P("section", None, "fsdp", None),
            P("section", None, None, None),
            P("section", None, None),
            P("section", None, None),
            P("section", None, None),
            P("section", None, None),
            P("section", None, None),
            P("section", None, "fsdp", None),
        ),
        out_specs=(
            P("section", "dp", "fsdp", None),
            P("section", "dp", "fsdp", None),
            P("section", None, None),
            P("section", None, "fsdp", None),
            P("section", None, None, None),
            P("section", None, None),
            P("section", None, None),
            P("section", None, None),
            P("section", None, None),
            P("section", None, None),
            P("section", None, "fsdp", None),
        ),
        check_vma=False,
    )
```

time: 3360 us -> 884 us (0.26)
  waiting for transfers between devices: 2360 us -> 0 us
  Pallas kernels: 0 us -> 807 us
  matrix products: 403 us -> 31 us
  other arithmetic: 268 us -> 14.4 us
  local copies, waits for them, and re-layouts: 224 us -> 17.9 us
  blocking collectives: 36.9 us -> 0 us
    unnamed x19 -> x0, waiting for transfers between devices: 990 us -> none
    all_gather x8 -> x0, waiting for transfers between devices: 829 us -> none  [the longest x1 332 us: fetch(): lax.all_gather(in_weight[0, depth_index], 'fsdp', axis=0, tiled=True)]
    pallas_call x0 -> x6, Pallas kernels: none -> 807 us  [the longest x2 263 us: run_layer_back(): pl.pallas_call(functools.partial(layer_back_kernel, ch, rows, nf, nd, las...]
    dot_general x54 -> x4, matrix products: 403 us -> 31 us  [dot(): lax.dot_general(a, b, (dims, ((), ())), preferred_element_type=F32, preci...]
    reduce_scatter x3 -> x0, waiting for transfers between devices: 286 us -> none  [layer_backward(): lax.psum_scatter(lax.dot_general(piece, grad_branch, (((0,), (0,)), ((),...]
    psum x2 -> x0, waiting for transfers between devices: 198 us -> none  [the longest x1 116 us: shards(): lax.psum(jnp.stack(in_sums).astype(jnp.bfloat16), 'dp').astype(jnp.float32)]
    unnamed x556 -> x22, local copies, waits for them, and re-layouts: 137 us -> 3.25 us
    reduce_sum x27 -> x6, other arithmetic: 86.6 us -> 1.66 us  [the longest x1 1.37 us: shards(): jnp.sum(in_all[:, 2 * ch:].astype(F32), axis=0)]
  transfers between devices with their start and end apart: 29 -> 0, of which waited for: 20 -> 0; matrix products, arithmetic and copies ran while one was open for 13% -> 0% of each run, Pallas kernels for 0% -> 0%
where the time goes in v1:
time: 884 us; the launch traced here: 872 us
  Pallas kernels  807 us (91%)
  matrix products  31 us (4%)
  local copies, waits for them, and re-layouts  17.9 us (2%)
  other arithmetic  14.4 us (2%)
    pallas_call x2, Pallas kernels, run_layer_back(): pl.pallas_call(functools.partial(layer_back_kernel, ch, rows, nf, nd, las...  263 us
    pallas_call x2, Pallas kernels, run_layer(): pl.pallas_call(functools.partial(layer_kernel, ch, rows, nf, nd, final),...  199 us
    pallas_call x1, Pallas kernels, run_start(): pl.pallas_call(functools.partial(start_kernel, nf, nd, rows), in_specs=[a...  174 us
    pallas_call x1, Pallas kernels, run_end(): pl.pallas_call(functools.partial(end_kernel, nf, nd), in_specs=[anywhere]...  172 us
    dot_general x4, matrix products, dot(): lax.dot_general(a, b, (dims, ((), ())), preferred_element_type=F32, preci...  31 us

profile of v1, /device:TPU:23, one launch (start us, length us, event | category | flops | bytes accessed | tf_op | source)
XLA Modules:
  0.0 871.7 jit_solution(10674763620419490840)
XLA Ops:
  0.6 0.7 dynamic-slice_convert_fusion
  1.3 1.3 select_maximum_fusion.head_ref
  2.6 0.6 broadcast_bitcast_fusion.seg_ref
  3.2 173.8 %gather_start.1 = (bf16[256,1536]{1,0:T(8,128)(2,1)}, bf16[1024,1536]{1,0:T(8,128)(2,1)}, bf16[4,1840,384]{2,1,0:T(8,128)(2,1)}, bf16[4,1840,384]{2,1,0:T(8,128)...) custom-call(bf16[2,256,1536]{2,1,0:T(8,128)(2,1)} %bitcast.72, ...), custom_call_target="tpu_custom_call" | custom-call | tf_op jit(solution)/shard_map/gather_start/pallas_call | solution.py:660
  177.0 1.4 slice.99.segrow_ref
  178.4 105.4 %layer_first.1 = (f32[1024,1840]{1,0:T(8,128)}, bf16[1024,768]{1,0:T(8,128)(2,1)}, f32[1024,768]{1,0:T(8,128)}, f32[1024,1024]{1,0:T(8,128)}, f32[8,128,768]{2,1...) custom-call(bf16[1024,1536]{1,0:T(8,128)(2,1)} %get-tuple-element.66, ...), custom_call_target="tpu_custom_call", output_to_operand_aliasing={{10}: (15, {})} | custom-call | tf_op jit(solution)/shard_map/layer_first/pallas_call | solution.py:1404
  283.8 93.4 %layer_last.1 = (f32[1024,1840]{1,0:T(8,128)}, bf16[1024,768]{1,0:T(8,128)(2,1)}, f32[1024,768]{1,0:T(8,128)}, f32[1024,1024]{1,0:T(8,128)}, f32[8,128,768]{2,1,...) custom-call(bf16[1024,1536]{1,0:T(8,128)(2,1)} %get-tuple-element.80, ...), custom_call_target="tpu_custom_call" | custom-call | tf_op jit(solution)/shard_map/layer_last/pallas_call | solution.py:1404
  377.2 6.5 convolution_convert_fusion.3.refs_0_
  383.7 0.0 copy-start.5
  383.8 0.0 copy-start.7
  383.8 139.2 %layer_back_first.1 = (bf16[1024,1840]{1,0:T(8,128)(2,1)}, f32[4,1024]{1,0:T(4,128)}, f32[8,1024]{1,0:T(8,128)}, f32[8,128]{1,0:T(8,128)}, f32[1,1536]{1,0:T(1,1...) custom-call(bf16[1024,1536]{1,0:T(8,128)(2,1)} %get-tuple-element.86., ...), custom_call_target="tpu_custom_call" | custom-call | tf_op jit(solution)/shard_map/layer_back_first/pallas_call | solution.py:1785
  523.0 0.8 slice_bitcast_fusion.1
  523.8 0.8 slice.81
  524.5 0.8 slice_reduce_fusion.3
  525.4 0.1 reshape_squeeze.7
  525.4 0.1 reduce_sum.55
  525.5 0.7 reduce.3
  526.3 0.7 copy.30
  527.0 0.1 concatenate.20
  527.1 0.0 copy-done.5
  527.1 0.0 copy-done.7
  527.1 0.0 copy-start.1
  527.1 0.0 copy-start.6
  527.1 6.1 convolution_convert_fusion.2.refs_0_
  533.2 0.0 copy-done.1
  533.2 0.0 copy-done.6
  533.2 8.2 convolution_convert_fusion.1.refs_1_
  541.3 0.0 copy-start
  541.3 124.0 %layer_back_last.1 = (bf16[1024,1840]{1,0:T(8,128)(2,1)}, f32[4,1024]{1,0:T(4,128)}, f32[8,1024]{1,0:T(8,128)}, f32[8,128]{1,0:T(8,128)}, f32[1,1536]{1,0:T(1,12...) custom-call(bf16[1024,1536]{1,0:T(8,128)(2,1)} %get-tuple-element.95, ...), custom_call_target="tpu_custom_call" | custom-call | tf_op jit(solution)/shard_map/layer_back_last/pallas_call | solution.py:1785
  665.3 0.8 slice_bitcast_fusion.3
  666.1 0.8 slice.76
  666.8 0.8 slice_reduce_fusion.5
  667.6 0.1 reshape_squeeze.6
  667.7 0.1 reduce_sum.54
  667.8 0.7 reduce
  668.6 0.7 copy.31
  669.3 0.1 concatenate.19
  669.4 0.6 pad_maximum_fusion.small_ref
  670.0 0.0 copy-done
  670.0 10.2 %convolution_convert_fusion.in_ref = bf16[1840,1536]{1,0:T(8,128)(2,1)} fusion(bf16[1024,1840]{1,0:T(8,128)(2,1)} %get-tuple-element.106, bf16[1024,1536]{1,0:T(8,128)(2,1)S(1)} %copy-done), kind=kOutput, calls=%fused_computation.1 | convolution fusion | flops 5790965760 | bytes 12566528 | tf_op jit(solution)/shard_map/dot_general | solution.py:27
  680.2 171.6 %sum_end.1 = (bf16[4,1840,384]{2,1,0:T(8,128)(2,1)}, bf16[768,1536]{1,0:T(8,128)(2,1)}, f32[256,128]{1,0:T(8,128)}) custom-call(bf16[1840,1536]{1,0:T(8,128)(2,1)} %convolution_convert_fusion.in_ref, bf16[928,384]{1,0:T(8,128)(2,1)} %get-tuple-element.107.in_part1_ref, bf16[192,768]{1,0:T(8,128)(2,1)} %get-tuple-element.108.out_part0_ref, ...), custom_call_target="tpu_custom_call" | custom-call | tf_op jit(solution)/shard_map/sum_end/pallas_call | solution.py:1058
  851.9 1.0 reshape.68
  852.9 0.1 fusion.4
  852.9 0.6 broadcast_in_dim_reshape.14
  853.5 0.6 broadcast_in_dim_reshape.13
  854.1 0.6 broadcast_in_dim_reshape.12
  854.7 0.6 broadcast_in_dim.32
  855.3 0.6 broadcast_in_dim_reshape.15
  856.0 0.6 broadcast_in_dim.35
  856.6 0.1 reshape.69
  856.7 0.6 maximum_bitcast_fusion.1
  857.3 1.4 convert_reduce_fusion
  858.7 2.9 fusion.2
  861.6 0.5 bitcast_convert_fusion.2
  862.2 0.5 bitcast_convert_fusion.1
  862.7 0.0 copy-start.2
  862.7 4.1 maximum_bitcast_fusion
  866.9 0.0 copy-done.2
  866.9 0.0 copy-start.3
  866.9 2.8 bitcast_convert_fusion
  869.7 0.0 copy-done.3
  869.7 0.9 copy.35
  870.6 0.0 copy-done.4
  870.6 0.9 copy.36
  (11 shorter events, 0.1 us)
Async XLA Ops:
  383.7 143.3 %copy-start.5 = (f32[8,128]{1,0:T(8,128)S(1)}, f32[8,128]{1,0:T(8,128)}, u32[]{:S(2)}) copy-start(f32[8,128]{1,0:T(8,128)} %get-tuple-element.100.ratio_ref) | copy-start | bytes 12292
  383.8 143.3 %copy-start.7 = (bf16[1024,768]{1,0:T(8,128)(2,1)S(1)}, bf16[1024,768]{1,0:T(8,128)(2,1)}, u32[]{:S(2)}) copy-start(bf16[1024,768]{1,0:T(8,128)(2,1)} %get-tuple-element.103) | copy-start | bytes 4718596
  527.1 6.1 copy-start.1
  527.1 6.1 copy-start.6
  541.3 128.7 %copy-start = (bf16[1024,1536]{1,0:T(8,128)(2,1)S(1)}, bf16[1024,1536]{1,0:T(8,128)(2,1)}, u32[]{:S(2)}) copy-start(bf16[1024,1536]{1,0:T(8,128)(2,1)} %get-tuple-element.66.normed_ref) | copy-start | bytes 9437188
  862.7 4.1 copy-start.2
  866.9 2.8 copy-start.3
  866.9 3.7 copy-start.4
